TPU v7x, 32 devices: a whole 2x2x4 slice. The times are simulated.
32 devices in a mesh: oct: 32 (over z, y, x, core).
Axes of the slice: x: 2, y: 2, z: 4, core: 2. Of those that a mesh axis runs over, the one named last changes fastest.
Arguments:
- leaf_spectra: bfloat16 [8192, 2016], P('oct'), may hold values from -6 to 6
- leaf_keys: int32 [8192], P('oct'), may hold values from 8 to 49159, as said below
- parent_keys: int32 [2048], P('oct'), may hold values from 1 to 6144, as said below
- child_phase: float32 [8, 1008], replicated, may hold values from -3.140625 to 3.140625
- coarsen: bfloat16 [2, 1008, 1008], replicated, may hold values from -0.0625 to 0.0625
- transfer: bfloat16 [316, 2016], replicated, may hold values from -0.3125 to 0.3125
- vlist_src: int32 [2048, 189], P('oct'), may hold values from -1 to 511, as said below
- vlist_type: int32 [2048, 189], P('oct'), may hold values from 0 to 315
Outputs:
- upward: bfloat16 [2048, 2016], P('oct')
- local_field: bfloat16 [2048, 2016], P('oct')
Inputs may be any that keep to these rules, and one draw needn't show every extreme that they name: leaf_keys: strictly increasing. Every leaf_keys // 8 is a value of parent_keys. The leaves of a parent lie on the device that owns it, except that some of the leaves of a device's last parent (at least one, at most two) are the first leaves of the next device; every device but the first begins so, and the last device's parents have all their leaves at home. parent_keys: strictly increasing; every parent has 1 to 8 leaves. `vlist_src`: in each row the live entries come first, then -1. A live entry is the index of a source parent within the target's window: the 512 parents that end with the last parent of the target's block of 64, counted cyclically. Every target has at least 94 live entries, and on every device some target has all 189 live.
All inputs are finite; a program needn't handle non-finite values.
Results may differ from a plain program's by a relative error of at most 0.0058.
Values may be sent and summed in bfloat16 or wider, within the bound.
A program may use at most 64 MiB of HBM per device.

v0:
```python
import jax
import jax.numpy as jnp
from jax import lax
from jax.sharding import PartitionSpec as P

GBITS = 3


def passed_along(value, axis, steps):
    count = lax.axis_size(axis)
    first, last = (max(0, -steps), min(count, count - steps))
    return lax.ppermute(value, axis, [(source, source + steps) for source in range(first, last)])


def from_behind(block, axis, distance):
    devices = range(lax.axis_size(axis))
    route = [((i - distance) % len(devices), i) for i in devices]
    return lax.ppermute(block, axis, route)


def interact(source_table, lower, sources, kinds, transfer, half_width):
    row_count = source_table.shape[0]
    slot_count = sources.shape[1]
    piece_width = -(-slot_count // 7)

    def one_piece(src_piece, kind_piece):
        local_index = src_piece - lower
        live_mask = (src_piece >= 0) & (local_index >= 0) & (local_index < row_count)

        def compute(unused):
            source_rows = source_table[jnp.clip(local_index, 0, row_count - 1)].astype(jnp.float32)
            coefficient = transfer[kind_piece].astype(jnp.float32)
            real_part = (
                coefficient[..., :half_width] * source_rows[..., :half_width]
                - coefficient[..., half_width:] * source_rows[..., half_width:]
            )
            imag_part = (
                coefficient[..., :half_width] * source_rows[..., half_width:]
                + coefficient[..., half_width:] * source_rows[..., :half_width]
            )
            products = jnp.concatenate([real_part, imag_part], -1)
            return jnp.sum(jnp.where(live_mask[..., None], products, jnp.float32(0.0)), 1)

        def nothing(unused):
            return jnp.zeros((src_piece.shape[0], 2 * half_width), jnp.float32)

        return lax.cond(jnp.any(live_mask), compute, nothing, 0)

    def one_block(block_pair):
        src_block, kind_block = block_pair
        total = jnp.zeros((src_block.shape[0], 2 * half_width), jnp.float32)
        for piece in range(7):
            total = total + one_piece(
                src_block[:, piece * piece_width : (piece + 1) * piece_width],
                kind_block[:, piece * piece_width : (piece + 1) * piece_width],
            )
        return total

    block_count = sources.shape[0] // 8
    results = lax.map(
        one_block, (sources.reshape(block_count, 8, -1), kinds.reshape(block_count, 8, -1))
    )
    return results.reshape(sources.shape[0], -1)


def shards(
    leaf_spectra, leaf_keys, parent_keys, child_phase, coarsen, transfer, vlist_src, vlist_type
):
    half_width = child_phase.shape[1]
    child_code = leaf_keys % 8
    parent_of = leaf_keys // 8
    phase_table = jnp.concatenate([jnp.cos(child_phase), jnp.sin(child_phase)], 1)
    picker = (child_code[:, None] == jnp.arange(8, dtype=jnp.int32)[None, :]).astype(jnp.float32)
    factors = jnp.dot(picker, phase_table, precision=lax.Precision.HIGHEST)
    cosine = factors[:, :half_width]
    sine_part = factors[:, half_width:]
    spectra = leaf_spectra.astype(jnp.float32)
    real_in = spectra[:, :half_width]
    imag_in = spectra[:, half_width:]
    twisted = jnp.concatenate(
        [real_in * cosine - imag_in * sine_part, real_in * sine_part + imag_in * cosine], 1
    )
    membership = (parent_of[:, None] == parent_keys[None, :]).astype(jnp.float32)
    gathered = jnp.einsum("lp,lc->pc", membership, twisted, precision=lax.Precision.HIGHEST)
    tail_mask = (parent_of < parent_keys[0]).astype(jnp.float32)
    tail_sum = jnp.dot(tail_mask, twisted, precision=lax.Precision.HIGHEST)
    incoming = passed_along(tail_sum, "oct", -1)
    gathered = jnp.concatenate([gathered[:-1], gathered[-1:] + incoming[None, :]], 0)
    gathered_b = gathered.astype(jnp.bfloat16)
    real_b = gathered_b[:, :half_width]
    imag_b = gathered_b[:, half_width:]
    real_out = jnp.dot(real_b, coarsen[0], preferred_element_type=jnp.float32) - jnp.dot(
        imag_b, coarsen[1], preferred_element_type=jnp.float32
    )
    imag_out = jnp.dot(real_b, coarsen[1], preferred_element_type=jnp.float32) + jnp.dot(
        imag_b, coarsen[0], preferred_element_type=jnp.float32
    )
    upward = jnp.concatenate([real_out, imag_out], 1).astype(jnp.bfloat16)
    window_count = 2**GBITS
    blocks = [upward]
    for distance in range(1, window_count):
        received = from_behind(upward, "oct", distance)
        blocks = [received] + blocks
    let_table = jnp.concatenate(blocks, 0)
    summed = interact(let_table, 0, vlist_src, vlist_type, transfer, half_width)
    local_field = summed.astype(jnp.bfloat16)
    return (upward, local_field)


def solution(mesh):
    return jax.shard_map(
        shards,
        mesh=mesh,
        in_specs=(
            P("oct", None),
            P("oct"),
            P("oct"),
            P(),
            P(),
            P(),
            P("oct", None),
            P("oct", None),
        ),
        out_specs=(P("oct", None), P("oct", None)),
        check_vma=False,
    )
```

profile of v0, /device:TPU:1, one launch (start us, length us, event | category | flops | bytes accessed | tf_op | source)
XLA Modules:
  0.0 1035.2 jit_solution(17076335462779935042)
XLA Ops:
  19.0 3.1 collective-permute-start.3
  27.0 3.4 collective-permute-start.6
  32.4 4.6 collective-permute-start.7
  41.0 10.3 collective-permute-done.5
  53.7 981.4 %while.10 = (s32[]{:T(128)}, bf16[8,8,2016]{2,1,0:T(8,128)(2,1)}, s32[8,8,189]{2,1,0:T(8,128)}, s32[8,8,189]{2,1,0:T(8,128)}, bf16[316,2016]{1,0:T(8,128)(2,1)S(1)}, /*index=5*/bf16[512,2016]{1,0:T(8,128)(2,1)S(1)}, s32[]{:T(128)}) while((s32[]{:T(128)}, bf16[8,8,2016]{2,1,0:T(8,128)(2,1)}, s32[8,8,189]{2,1,0:T(8,128)}, ...), condition=%wide.region_29.30_spmd, body=%wide.region_0.29_spmd.sunk | while | flops 18305504 | bytes 110904272 | solution.py:60
  57.5 13.4 %conditional.15 = (f32[8,2016]{1,0:T(8,128)S(1)}) conditional(s32[]{:T(128)} %convert_element_type.103, () %tuple.129, (pred[8,27]{1,0:T(8,128)(4,1)S(1)}, s32[8,189]{1,0:T(8,128)S(1)}, bf16[316,2016]{1,0:T(8,128)(2,1)S(1)}, s32[8,27]{1,0:T(8,128)S(1)}, bf16[512,2016]{1,0:T(8,128)(2,1)S(1)}) %tuple.130), branch_computations={%region_22.22_spmd, %region_23.24_spmd} | conditional | flops 2600168 | bytes 15759712 | solution.py:47
  71.4 14.1 %conditional.16 = (f32[8,2016]{1,0:T(8,128)S(1)}) conditional(s32[]{:T(128)} %convert_element_type.104, () %tuple.131, (pred[8,27]{1,0:T(8,128)(4,1)}, s32[8,189]{1,0:T(8,128)S(1)}, bf16[316,2016]{1,0:T(8,128)(2,1)S(1)}, s32[8,27]{1,0:T(8,128)}, bf16[512,2016]{1,0:T(8,128)(2,1)S(1)}) %tuple.132), branch_computations={%region_18.18_spmd, %region_19.20_spmd} | conditional | flops 2600168 | bytes 15760604 | solution.py:47
  82.1 2.9 multiply_subtract_fusion.4
  86.2 17.8 %conditional.17 = (f32[8,2016]{1,0:T(8,128)}) conditional(s32[]{:T(128)} %convert_element_type.105, () %tuple.133, (pred[8,27]{1,0:T(8,128)(4,1)}, s32[8,189]{1,0:T(8,128)S(1)}, bf16[316,2016]{1,0:T(8,128)(2,1)S(1)}, s32[8,27]{1,0:T(8,128)S(1)}, bf16[512,2016]{1,0:T(8,128)(2,1)S(1)}) %tuple.134), branch_computations={%region_14.14_spmd, %region_15.16_spmd} | conditional | flops 2600168 | bytes 15764088 | solution.py:47
  104.7 17.7 %conditional.18 = (f32[8,2016]{1,0:T(8,128)}) conditional(s32[]{:T(128)} %convert_element_type.106, () %tuple.135, (pred[8,27]{1,0:T(8,128)(4,1)}, s32[8,189]{1,0:T(8,128)S(1)}, bf16[316,2016]{1,0:T(8,128)(2,1)S(1)}, s32[8,27]{1,0:T(8,128)}, bf16[512,2016]{1,0:T(8,128)(2,1)S(1)}) %tuple.136), branch_computations={%region_10.10_spmd, %region_11.12_spmd} | conditional | flops 2600168 | bytes 15764088 | solution.py:47
  123.1 17.6 %conditional.19 = (f32[8,2016]{1,0:T(8,128)}) conditional(s32[]{:T(128)} %convert_element_type.107, () %tuple.137, (pred[8,27]{1,0:T(8,128)(4,1)}, s32[8,189]{1,0:T(8,128)S(1)}, bf16[316,2016]{1,0:T(8,128)(2,1)S(1)}, s32[8,27]{1,0:T(8,128)}, bf16[512,2016]{1,0:T(8,128)(2,1)S(1)}) %tuple.138), branch_computations={%region_2.2_spmd, %region_3.4_spmd} | conditional | flops 2600168 | bytes 15764088 | solution.py:47
  136.6 2.9 multiply_subtract_fusion
  141.3 17.7 %conditional.20 = (f32[8,2016]{1,0:T(8,128)}) conditional(s32[]{:T(128)} %convert_element_type.108, () %tuple.139, (pred[8,27]{1,0:T(8,128)(4,1)}, s32[8,189]{1,0:T(8,128)S(1)}, bf16[316,2016]{1,0:T(8,128)(2,1)S(1)}, s32[8,27]{1,0:T(8,128)}, bf16[512,2016]{1,0:T(8,128)(2,1)S(1)}) %tuple.140), branch_computations={%region_6.6_spmd, %region_7.8_spmd} | conditional | flops 2600168 | bytes 15764088 | solution.py:47
  159.7 15.3 %conditional.14 = (f32[8,2016]{1,0:T(8,128)}) conditional(s32[]{:T(128)} %convert_element_type.102, () %tuple.127, (pred[8,27]{1,0:T(8,128)(4,1)}, s32[8,189]{1,0:T(8,128)S(1)}, bf16[316,2016]{1,0:T(8,128)(2,1)S(1)}, s32[8,27]{1,0:T(8,128)S(1)}, bf16[512,2016]{1,0:T(8,128)(2,1)S(1)}) %tuple.128), branch_computations={%region_26.26_spmd, %region_27.28_spmd} | conditional | flops 2600168 | bytes 15760604 | solution.py:47
  180.1 13.4 %conditional.15 = (f32[8,2016]{1,0:T(8,128)S(1)}) conditional(s32[]{:T(128)} %convert_element_type.103, () %tuple.129, (pred[8,27]{1,0:T(8,128)(4,1)S(1)}, s32[8,189]{1,0:T(8,128)S(1)}, bf16[316,2016]{1,0:T(8,128)(2,1)S(1)}, s32[8,27]{1,0:T(8,128)S(1)}, bf16[512,2016]{1,0:T(8,128)(2,1)S(1)}) %tuple.130), branch_computations={%region_22.22_spmd, %region_23.24_spmd} | conditional | flops 2600168 | bytes 15759712 | solution.py:47
  194.1 14.1 %conditional.16 = (f32[8,2016]{1,0:T(8,128)S(1)}) conditional(s32[]{:T(128)} %convert_element_type.104, () %tuple.131, (pred[8,27]{1,0:T(8,128)(4,1)}, s32[8,189]{1,0:T(8,128)S(1)}, bf16[316,2016]{1,0:T(8,128)(2,1)S(1)}, s32[8,27]{1,0:T(8,128)}, bf16[512,2016]{1,0:T(8,128)(2,1)S(1)}) %tuple.132), branch_computations={%region_18.18_spmd, %region_19.20_spmd} | conditional | flops 2600168 | bytes 15760604 | solution.py:47
  208.9 17.8 %conditional.17 = (f32[8,2016]{1,0:T(8,128)}) conditional(s32[]{:T(128)} %convert_element_type.105, () %tuple.133, (pred[8,27]{1,0:T(8,128)(4,1)}, s32[8,189]{1,0:T(8,128)S(1)}, bf16[316,2016]{1,0:T(8,128)(2,1)S(1)}, s32[8,27]{1,0:T(8,128)S(1)}, bf16[512,2016]{1,0:T(8,128)(2,1)S(1)}) %tuple.134), branch_computations={%region_14.14_spmd, %region_15.16_spmd} | conditional | flops 2600168 | bytes 15764088 | solution.py:47
  222.6 2.9 multiply_subtract_fusion.3
  227.4 17.7 %conditional.18 = (f32[8,2016]{1,0:T(8,128)}) conditional(s32[]{:T(128)} %convert_element_type.106, () %tuple.135, (pred[8,27]{1,0:T(8,128)(4,1)}, s32[8,189]{1,0:T(8,128)S(1)}, bf16[316,2016]{1,0:T(8,128)(2,1)S(1)}, s32[8,27]{1,0:T(8,128)}, bf16[512,2016]{1,0:T(8,128)(2,1)S(1)}) %tuple.136), branch_computations={%region_10.10_spmd, %region_11.12_spmd} | conditional | flops 2600168 | bytes 15764088 | solution.py:47
  245.7 17.6 %conditional.19 = (f32[8,2016]{1,0:T(8,128)}) conditional(s32[]{:T(128)} %convert_element_type.107, () %tuple.137, (pred[8,27]{1,0:T(8,128)(4,1)}, s32[8,189]{1,0:T(8,128)S(1)}, bf16[316,2016]{1,0:T(8,128)(2,1)S(1)}, s32[8,27]{1,0:T(8,128)}, bf16[512,2016]{1,0:T(8,128)(2,1)S(1)}) %tuple.138), branch_computations={%region_2.2_spmd, %region_3.4_spmd} | conditional | flops 2600168 | bytes 15764088 | solution.py:47
  264.0 17.7 %conditional.20 = (f32[8,2016]{1,0:T(8,128)}) conditional(s32[]{:T(128)} %convert_element_type.108, () %tuple.139, (pred[8,27]{1,0:T(8,128)(4,1)}, s32[8,189]{1,0:T(8,128)S(1)}, bf16[316,2016]{1,0:T(8,128)(2,1)S(1)}, s32[8,27]{1,0:T(8,128)}, bf16[512,2016]{1,0:T(8,128)(2,1)S(1)}) %tuple.140), branch_computations={%region_6.6_spmd, %region_7.8_spmd} | conditional | flops 2600168 | bytes 15764088 | solution.py:47
  282.3 15.3 %conditional.14 = (f32[8,2016]{1,0:T(8,128)}) conditional(s32[]{:T(128)} %convert_element_type.102, () %tuple.127, (pred[8,27]{1,0:T(8,128)(4,1)}, s32[8,189]{1,0:T(8,128)S(1)}, bf16[316,2016]{1,0:T(8,128)(2,1)S(1)}, s32[8,27]{1,0:T(8,128)S(1)}, bf16[512,2016]{1,0:T(8,128)(2,1)S(1)}) %tuple.128), branch_computations={%region_26.26_spmd, %region_27.28_spmd} | conditional | flops 2600168 | bytes 15760604 | solution.py:47
  302.8 13.4 %conditional.15 = (f32[8,2016]{1,0:T(8,128)S(1)}) conditional(s32[]{:T(128)} %convert_element_type.103, () %tuple.129, (pred[8,27]{1,0:T(8,128)(4,1)S(1)}, s32[8,189]{1,0:T(8,128)S(1)}, bf16[316,2016]{1,0:T(8,128)(2,1)S(1)}, s32[8,27]{1,0:T(8,128)S(1)}, bf16[512,2016]{1,0:T(8,128)(2,1)S(1)}) %tuple.130), branch_computations={%region_22.22_spmd, %region_23.24_spmd} | conditional | flops 2600168 | bytes 15759712 | solution.py:47
  316.8 14.1 %conditional.16 = (f32[8,2016]{1,0:T(8,128)S(1)}) conditional(s32[]{:T(128)} %convert_element_type.104, () %tuple.131, (pred[8,27]{1,0:T(8,128)(4,1)}, s32[8,189]{1,0:T(8,128)S(1)}, bf16[316,2016]{1,0:T(8,128)(2,1)S(1)}, s32[8,27]{1,0:T(8,128)}, bf16[512,2016]{1,0:T(8,128)(2,1)S(1)}) %tuple.132), branch_computations={%region_18.18_spmd, %region_19.20_spmd} | conditional | flops 2600168 | bytes 15760604 | solution.py:47
  331.5 17.8 %conditional.17 = (f32[8,2016]{1,0:T(8,128)}) conditional(s32[]{:T(128)} %convert_element_type.105, () %tuple.133, (pred[8,27]{1,0:T(8,128)(4,1)}, s32[8,189]{1,0:T(8,128)S(1)}, bf16[316,2016]{1,0:T(8,128)(2,1)S(1)}, s32[8,27]{1,0:T(8,128)S(1)}, bf16[512,2016]{1,0:T(8,128)(2,1)S(1)}) %tuple.134), branch_computations={%region_14.14_spmd, %region_15.16_spmd} | conditional | flops 2600168 | bytes 15764088 | solution.py:47
  350.0 17.7 %conditional.18 = (f32[8,2016]{1,0:T(8,128)}) conditional(s32[]{:T(128)} %convert_element_type.106, () %tuple.135, (pred[8,27]{1,0:T(8,128)(4,1)}, s32[8,189]{1,0:T(8,128)S(1)}, bf16[316,2016]{1,0:T(8,128)(2,1)S(1)}, s32[8,27]{1,0:T(8,128)}, bf16[512,2016]{1,0:T(8,128)(2,1)S(1)}) %tuple.136), branch_computations={%region_10.10_spmd, %region_11.12_spmd} | conditional | flops 2600168 | bytes 15764088 | solution.py:47
  368.4 17.6 %conditional.19 = (f32[8,2016]{1,0:T(8,128)}) conditional(s32[]{:T(128)} %convert_element_type.107, () %tuple.137, (pred[8,27]{1,0:T(8,128)(4,1)}, s32[8,189]{1,0:T(8,128)S(1)}, bf16[316,2016]{1,0:T(8,128)(2,1)S(1)}, s32[8,27]{1,0:T(8,128)}, bf16[512,2016]{1,0:T(8,128)(2,1)S(1)}) %tuple.138), branch_computations={%region_2.2_spmd, %region_3.4_spmd} | conditional | flops 2600168 | bytes 15764088 | solution.py:47
  386.6 17.7 %conditional.20 = (f32[8,2016]{1,0:T(8,128)}) conditional(s32[]{:T(128)} %convert_element_type.108, () %tuple.139, (pred[8,27]{1,0:T(8,128)(4,1)}, s32[8,189]{1,0:T(8,128)S(1)}, bf16[316,2016]{1,0:T(8,128)(2,1)S(1)}, s32[8,27]{1,0:T(8,128)}, bf16[512,2016]{1,0:T(8,128)(2,1)S(1)}) %tuple.140), branch_computations={%region_6.6_spmd, %region_7.8_spmd} | conditional | flops 2600168 | bytes 15764088 | solution.py:47
  405.0 15.3 %conditional.14 = (f32[8,2016]{1,0:T(8,128)}) conditional(s32[]{:T(128)} %convert_element_type.102, () %tuple.127, (pred[8,27]{1,0:T(8,128)(4,1)}, s32[8,189]{1,0:T(8,128)S(1)}, bf16[316,2016]{1,0:T(8,128)(2,1)S(1)}, s32[8,27]{1,0:T(8,128)S(1)}, bf16[512,2016]{1,0:T(8,128)(2,1)S(1)}) %tuple.128), branch_computations={%region_26.26_spmd, %region_27.28_spmd} | conditional | flops 2600168 | bytes 15760604 | solution.py:47
  425.4 13.4 %conditional.15 = (f32[8,2016]{1,0:T(8,128)S(1)}) conditional(s32[]{:T(128)} %convert_element_type.103, () %tuple.129, (pred[8,27]{1,0:T(8,128)(4,1)S(1)}, s32[8,189]{1,0:T(8,128)S(1)}, bf16[316,2016]{1,0:T(8,128)(2,1)S(1)}, s32[8,27]{1,0:T(8,128)S(1)}, bf16[512,2016]{1,0:T(8,128)(2,1)S(1)}) %tuple.130), branch_computations={%region_22.22_spmd, %region_23.24_spmd} | conditional | flops 2600168 | bytes 15759712 | solution.py:47
  439.4 14.1 %conditional.16 = (f32[8,2016]{1,0:T(8,128)S(1)}) conditional(s32[]{:T(128)} %convert_element_type.104, () %tuple.131, (pred[8,27]{1,0:T(8,128)(4,1)}, s32[8,189]{1,0:T(8,128)S(1)}, bf16[316,2016]{1,0:T(8,128)(2,1)S(1)}, s32[8,27]{1,0:T(8,128)}, bf16[512,2016]{1,0:T(8,128)(2,1)S(1)}) %tuple.132), branch_computations={%region_18.18_spmd, %region_19.20_spmd} | conditional | flops 2600168 | bytes 15760604 | solution.py:47
  454.2 17.8 %conditional.17 = (f32[8,2016]{1,0:T(8,128)}) conditional(s32[]{:T(128)} %convert_element_type.105, () %tuple.133, (pred[8,27]{1,0:T(8,128)(4,1)}, s32[8,189]{1,0:T(8,128)S(1)}, bf16[316,2016]{1,0:T(8,128)(2,1)S(1)}, s32[8,27]{1,0:T(8,128)S(1)}, bf16[512,2016]{1,0:T(8,128)(2,1)S(1)}) %tuple.134), branch_computations={%region_14.14_spmd, %region_15.16_spmd} | conditional | flops 2600168 | bytes 15764088 | solution.py:47
  472.7 17.7 %conditional.18 = (f32[8,2016]{1,0:T(8,128)}) conditional(s32[]{:T(128)} %convert_element_type.106, () %tuple.135, (pred[8,27]{1,0:T(8,128)(4,1)}, s32[8,189]{1,0:T(8,128)S(1)}, bf16[316,2016]{1,0:T(8,128)(2,1)S(1)}, s32[8,27]{1,0:T(8,128)}, bf16[512,2016]{1,0:T(8,128)(2,1)S(1)}) %tuple.136), branch_computations={%region_10.10_spmd, %region_11.12_spmd} | conditional | flops 2600168 | bytes 15764088 | solution.py:47
  491.0 17.6 %conditional.19 = (f32[8,2016]{1,0:T(8,128)}) conditional(s32[]{:T(128)} %convert_element_type.107, () %tuple.137, (pred[8,27]{1,0:T(8,128)(4,1)}, s32[8,189]{1,0:T(8,128)S(1)}, bf16[316,2016]{1,0:T(8,128)(2,1)S(1)}, s32[8,27]{1,0:T(8,128)}, bf16[512,2016]{1,0:T(8,128)(2,1)S(1)}) %tuple.138), branch_computations={%region_2.2_spmd, %region_3.4_spmd} | conditional | flops 2600168 | bytes 15764088 | solution.py:47
  509.3 17.7 %conditional.20 = (f32[8,2016]{1,0:T(8,128)}) conditional(s32[]{:T(128)} %convert_element_type.108, () %tuple.139, (pred[8,27]{1,0:T(8,128)(4,1)}, s32[8,189]{1,0:T(8,128)S(1)}, bf16[316,2016]{1,0:T(8,128)(2,1)S(1)}, s32[8,27]{1,0:T(8,128)}, bf16[512,2016]{1,0:T(8,128)(2,1)S(1)}) %tuple.140), branch_computations={%region_6.6_spmd, %region_7.8_spmd} | conditional | flops 2600168 | bytes 15764088 | solution.py:47
  527.6 15.3 %conditional.14 = (f32[8,2016]{1,0:T(8,128)}) conditional(s32[]{:T(128)} %convert_element_type.102, () %tuple.127, (pred[8,27]{1,0:T(8,128)(4,1)}, s32[8,189]{1,0:T(8,128)S(1)}, bf16[316,2016]{1,0:T(8,128)(2,1)S(1)}, s32[8,27]{1,0:T(8,128)S(1)}, bf16[512,2016]{1,0:T(8,128)(2,1)S(1)}) %tuple.128), branch_computations={%region_26.26_spmd, %region_27.28_spmd} | conditional | flops 2600168 | bytes 15760604 | solution.py:47
  548.1 13.4 %conditional.15 = (f32[8,2016]{1,0:T(8,128)S(1)}) conditional(s32[]{:T(128)} %convert_element_type.103, () %tuple.129, (pred[8,27]{1,0:T(8,128)(4,1)S(1)}, s32[8,189]{1,0:T(8,128)S(1)}, bf16[316,2016]{1,0:T(8,128)(2,1)S(1)}, s32[8,27]{1,0:T(8,128)S(1)}, bf16[512,2016]{1,0:T(8,128)(2,1)S(1)}) %tuple.130), branch_computations={%region_22.22_spmd, %region_23.24_spmd} | conditional | flops 2600168 | bytes 15759712 | solution.py:47
  562.1 14.1 %conditional.16 = (f32[8,2016]{1,0:T(8,128)S(1)}) conditional(s32[]{:T(128)} %convert_element_type.104, () %tuple.131, (pred[8,27]{1,0:T(8,128)(4,1)}, s32[8,189]{1,0:T(8,128)S(1)}, bf16[316,2016]{1,0:T(8,128)(2,1)S(1)}, s32[8,27]{1,0:T(8,128)}, bf16[512,2016]{1,0:T(8,128)(2,1)S(1)}) %tuple.132), branch_computations={%region_18.18_spmd, %region_19.20_spmd} | conditional | flops 2600168 | bytes 15760604 | solution.py:47
  576.8 17.8 %conditional.17 = (f32[8,2016]{1,0:T(8,128)}) conditional(s32[]{:T(128)} %convert_element_type.105, () %tuple.133, (pred[8,27]{1,0:T(8,128)(4,1)}, s32[8,189]{1,0:T(8,128)S(1)}, bf16[316,2016]{1,0:T(8,128)(2,1)S(1)}, s32[8,27]{1,0:T(8,128)S(1)}, bf16[512,2016]{1,0:T(8,128)(2,1)S(1)}) %tuple.134), branch_computations={%region_14.14_spmd, %region_15.16_spmd} | conditional | flops 2600168 | bytes 15764088 | solution.py:47
  595.3 17.7 %conditional.18 = (f32[8,2016]{1,0:T(8,128)}) conditional(s32[]{:T(128)} %convert_element_type.106, () %tuple.135, (pred[8,27]{1,0:T(8,128)(4,1)}, s32[8,189]{1,0:T(8,128)S(1)}, bf16[316,2016]{1,0:T(8,128)(2,1)S(1)}, s32[8,27]{1,0:T(8,128)}, bf16[512,2016]{1,0:T(8,128)(2,1)S(1)}) %tuple.136), branch_computations={%region_10.10_spmd, %region_11.12_spmd} | conditional | flops 2600168 | bytes 15764088 | solution.py:47
  613.7 17.6 %conditional.19 = (f32[8,2016]{1,0:T(8,128)}) conditional(s32[]{:T(128)} %convert_element_type.107, () %tuple.137, (pred[8,27]{1,0:T(8,128)(4,1)}, s32[8,189]{1,0:T(8,128)S(1)}, bf16[316,2016]{1,0:T(8,128)(2,1)S(1)}, s32[8,27]{1,0:T(8,128)}, bf16[512,2016]{1,0:T(8,128)(2,1)S(1)}) %tuple.138), branch_computations={%region_2.2_spmd, %region_3.4_spmd} | conditional | flops 2600168 | bytes 15764088 | solution.py:47
  631.9 17.7 %conditional.20 = (f32[8,2016]{1,0:T(8,128)}) conditional(s32[]{:T(128)} %convert_element_type.108, () %tuple.139, (pred[8,27]{1,0:T(8,128)(4,1)}, s32[8,189]{1,0:T(8,128)S(1)}, bf16[316,2016]{1,0:T(8,128)(2,1)S(1)}, s32[8,27]{1,0:T(8,128)}, bf16[512,2016]{1,0:T(8,128)(2,1)S(1)}) %tuple.140), branch_computations={%region_6.6_spmd, %region_7.8_spmd} | conditional | flops 2600168 | bytes 15764088 | solution.py:47
  650.3 15.3 %conditional.14 = (f32[8,2016]{1,0:T(8,128)}) conditional(s32[]{:T(128)} %convert_element_type.102, () %tuple.127, (pred[8,27]{1,0:T(8,128)(4,1)}, s32[8,189]{1,0:T(8,128)S(1)}, bf16[316,2016]{1,0:T(8,128)(2,1)S(1)}, s32[8,27]{1,0:T(8,128)S(1)}, bf16[512,2016]{1,0:T(8,128)(2,1)S(1)}) %tuple.128), branch_computations={%region_26.26_spmd, %region_27.28_spmd} | conditional | flops 2600168 | bytes 15760604 | solution.py:47
  670.7 13.4 %conditional.15 = (f32[8,2016]{1,0:T(8,128)S(1)}) conditional(s32[]{:T(128)} %convert_element_type.103, () %tuple.129, (pred[8,27]{1,0:T(8,128)(4,1)S(1)}, s32[8,189]{1,0:T(8,128)S(1)}, bf16[316,2016]{1,0:T(8,128)(2,1)S(1)}, s32[8,27]{1,0:T(8,128)S(1)}, bf16[512,2016]{1,0:T(8,128)(2,1)S(1)}) %tuple.130), branch_computations={%region_22.22_spmd, %region_23.24_spmd} | conditional | flops 2600168 | bytes 15759712 | solution.py:47
  684.7 14.1 %conditional.16 = (f32[8,2016]{1,0:T(8,128)S(1)}) conditional(s32[]{:T(128)} %convert_element_type.104, () %tuple.131, (pred[8,27]{1,0:T(8,128)(4,1)}, s32[8,189]{1,0:T(8,128)S(1)}, bf16[316,2016]{1,0:T(8,128)(2,1)S(1)}, s32[8,27]{1,0:T(8,128)}, bf16[512,2016]{1,0:T(8,128)(2,1)S(1)}) %tuple.132), branch_computations={%region_18.18_spmd, %region_19.20_spmd} | conditional | flops 2600168 | bytes 15760604 | solution.py:47
  699.5 17.8 %conditional.17 = (f32[8,2016]{1,0:T(8,128)}) conditional(s32[]{:T(128)} %convert_element_type.105, () %tuple.133, (pred[8,27]{1,0:T(8,128)(4,1)}, s32[8,189]{1,0:T(8,128)S(1)}, bf16[316,2016]{1,0:T(8,128)(2,1)S(1)}, s32[8,27]{1,0:T(8,128)S(1)}, bf16[512,2016]{1,0:T(8,128)(2,1)S(1)}) %tuple.134), branch_computations={%region_14.14_spmd, %region_15.16_spmd} | conditional | flops 2600168 | bytes 15764088 | solution.py:47
  718.0 17.7 %conditional.18 = (f32[8,2016]{1,0:T(8,128)}) conditional(s32[]{:T(128)} %convert_element_type.106, () %tuple.135, (pred[8,27]{1,0:T(8,128)(4,1)}, s32[8,189]{1,0:T(8,128)S(1)}, bf16[316,2016]{1,0:T(8,128)(2,1)S(1)}, s32[8,27]{1,0:T(8,128)}, bf16[512,2016]{1,0:T(8,128)(2,1)S(1)}) %tuple.136), branch_computations={%region_10.10_spmd, %region_11.12_spmd} | conditional | flops 2600168 | bytes 15764088 | solution.py:47
  736.3 17.6 %conditional.19 = (f32[8,2016]{1,0:T(8,128)}) conditional(s32[]{:T(128)} %convert_element_type.107, () %tuple.137, (pred[8,27]{1,0:T(8,128)(4,1)}, s32[8,189]{1,0:T(8,128)S(1)}, bf16[316,2016]{1,0:T(8,128)(2,1)S(1)}, s32[8,27]{1,0:T(8,128)}, bf16[512,2016]{1,0:T(8,128)(2,1)S(1)}) %tuple.138), branch_computations={%region_2.2_spmd, %region_3.4_spmd} | conditional | flops 2600168 | bytes 15764088 | solution.py:47
  754.6 17.7 %conditional.20 = (f32[8,2016]{1,0:T(8,128)}) conditional(s32[]{:T(128)} %convert_element_type.108, () %tuple.139, (pred[8,27]{1,0:T(8,128)(4,1)}, s32[8,189]{1,0:T(8,128)S(1)}, bf16[316,2016]{1,0:T(8,128)(2,1)S(1)}, s32[8,27]{1,0:T(8,128)}, bf16[512,2016]{1,0:T(8,128)(2,1)S(1)}) %tuple.140), branch_computations={%region_6.6_spmd, %region_7.8_spmd} | conditional | flops 2600168 | bytes 15764088 | solution.py:47
  772.9 15.3 %conditional.14 = (f32[8,2016]{1,0:T(8,128)}) conditional(s32[]{:T(128)} %convert_element_type.102, () %tuple.127, (pred[8,27]{1,0:T(8,128)(4,1)}, s32[8,189]{1,0:T(8,128)S(1)}, bf16[316,2016]{1,0:T(8,128)(2,1)S(1)}, s32[8,27]{1,0:T(8,128)S(1)}, bf16[512,2016]{1,0:T(8,128)(2,1)S(1)}) %tuple.128), branch_computations={%region_26.26_spmd, %region_27.28_spmd} | conditional | flops 2600168 | bytes 15760604 | solution.py:47
  793.4 13.4 %conditional.15 = (f32[8,2016]{1,0:T(8,128)S(1)}) conditional(s32[]{:T(128)} %convert_element_type.103, () %tuple.129, (pred[8,27]{1,0:T(8,128)(4,1)S(1)}, s32[8,189]{1,0:T(8,128)S(1)}, bf16[316,2016]{1,0:T(8,128)(2,1)S(1)}, s32[8,27]{1,0:T(8,128)S(1)}, bf16[512,2016]{1,0:T(8,128)(2,1)S(1)}) %tuple.130), branch_computations={%region_22.22_spmd, %region_23.24_spmd} | conditional | flops 2600168 | bytes 15759712 | solution.py:47
  807.4 14.1 %conditional.16 = (f32[8,2016]{1,0:T(8,128)S(1)}) conditional(s32[]{:T(128)} %convert_element_type.104, () %tuple.131, (pred[8,27]{1,0:T(8,128)(4,1)}, s32[8,189]{1,0:T(8,128)S(1)}, bf16[316,2016]{1,0:T(8,128)(2,1)S(1)}, s32[8,27]{1,0:T(8,128)}, bf16[512,2016]{1,0:T(8,128)(2,1)S(1)}) %tuple.132), branch_computations={%region_18.18_spmd, %region_19.20_spmd} | conditional | flops 2600168 | bytes 15760604 | solution.py:47
  822.1 17.8 %conditional.17 = (f32[8,2016]{1,0:T(8,128)}) conditional(s32[]{:T(128)} %convert_element_type.105, () %tuple.133, (pred[8,27]{1,0:T(8,128)(4,1)}, s32[8,189]{1,0:T(8,128)S(1)}, bf16[316,2016]{1,0:T(8,128)(2,1)S(1)}, s32[8,27]{1,0:T(8,128)S(1)}, bf16[512,2016]{1,0:T(8,128)(2,1)S(1)}) %tuple.134), branch_computations={%region_14.14_spmd, %region_15.16_spmd} | conditional | flops 2600168 | bytes 15764088 | solution.py:47
  840.7 17.7 %conditional.18 = (f32[8,2016]{1,0:T(8,128)}) conditional(s32[]{:T(128)} %convert_element_type.106, () %tuple.135, (pred[8,27]{1,0:T(8,128)(4,1)}, s32[8,189]{1,0:T(8,128)S(1)}, bf16[316,2016]{1,0:T(8,128)(2,1)S(1)}, s32[8,27]{1,0:T(8,128)}, bf16[512,2016]{1,0:T(8,128)(2,1)S(1)}) %tuple.136), branch_computations={%region_10.10_spmd, %region_11.12_spmd} | conditional | flops 2600168 | bytes 15764088 | solution.py:47
  859.0 17.6 %conditional.19 = (f32[8,2016]{1,0:T(8,128)}) conditional(s32[]{:T(128)} %convert_element_type.107, () %tuple.137, (pred[8,27]{1,0:T(8,128)(4,1)}, s32[8,189]{1,0:T(8,128)S(1)}, bf16[316,2016]{1,0:T(8,128)(2,1)S(1)}, s32[8,27]{1,0:T(8,128)}, bf16[512,2016]{1,0:T(8,128)(2,1)S(1)}) %tuple.138), branch_computations={%region_2.2_spmd, %region_3.4_spmd} | conditional | flops 2600168 | bytes 15764088 | solution.py:47
  877.2 17.7 %conditional.20 = (f32[8,2016]{1,0:T(8,128)}) conditional(s32[]{:T(128)} %convert_element_type.108, () %tuple.139, (pred[8,27]{1,0:T(8,128)(4,1)}, s32[8,189]{1,0:T(8,128)S(1)}, bf16[316,2016]{1,0:T(8,128)(2,1)S(1)}, s32[8,27]{1,0:T(8,128)}, bf16[512,2016]{1,0:T(8,128)(2,1)S(1)}) %tuple.140), branch_computations={%region_6.6_spmd, %region_7.8_spmd} | conditional | flops 2600168 | bytes 15764088 | solution.py:47
  895.6 15.3 %conditional.14 = (f32[8,2016]{1,0:T(8,128)}) conditional(s32[]{:T(128)} %convert_element_type.102, () %tuple.127, (pred[8,27]{1,0:T(8,128)(4,1)}, s32[8,189]{1,0:T(8,128)S(1)}, bf16[316,2016]{1,0:T(8,128)(2,1)S(1)}, s32[8,27]{1,0:T(8,128)S(1)}, bf16[512,2016]{1,0:T(8,128)(2,1)S(1)}) %tuple.128), branch_computations={%region_26.26_spmd, %region_27.28_spmd} | conditional | flops 2600168 | bytes 15760604 | solution.py:47
  916.1 13.4 %conditional.15 = (f32[8,2016]{1,0:T(8,128)S(1)}) conditional(s32[]{:T(128)} %convert_element_type.103, () %tuple.129, (pred[8,27]{1,0:T(8,128)(4,1)S(1)}, s32[8,189]{1,0:T(8,128)S(1)}, bf16[316,2016]{1,0:T(8,128)(2,1)S(1)}, s32[8,27]{1,0:T(8,128)S(1)}, bf16[512,2016]{1,0:T(8,128)(2,1)S(1)}) %tuple.130), branch_computations={%region_22.22_spmd, %region_23.24_spmd} | conditional | flops 2600168 | bytes 15759712 | solution.py:47
  930.0 14.1 %conditional.16 = (f32[8,2016]{1,0:T(8,128)S(1)}) conditional(s32[]{:T(128)} %convert_element_type.104, () %tuple.131, (pred[8,27]{1,0:T(8,128)(4,1)}, s32[8,189]{1,0:T(8,128)S(1)}, bf16[316,2016]{1,0:T(8,128)(2,1)S(1)}, s32[8,27]{1,0:T(8,128)}, bf16[512,2016]{1,0:T(8,128)(2,1)S(1)}) %tuple.132), branch_computations={%region_18.18_spmd, %region_19.20_spmd} | conditional | flops 2600168 | bytes 15760604 | solution.py:47
  944.8 17.8 %conditional.17 = (f32[8,2016]{1,0:T(8,128)}) conditional(s32[]{:T(128)} %convert_element_type.105, () %tuple.133, (pred[8,27]{1,0:T(8,128)(4,1)}, s32[8,189]{1,0:T(8,128)S(1)}, bf16[316,2016]{1,0:T(8,128)(2,1)S(1)}, s32[8,27]{1,0:T(8,128)S(1)}, bf16[512,2016]{1,0:T(8,128)(2,1)S(1)}) %tuple.134), branch_computations={%region_14.14_spmd, %region_15.16_spmd} | conditional | flops 2600168 | bytes 15764088 | solution.py:47
  963.3 17.7 %conditional.18 = (f32[8,2016]{1,0:T(8,128)}) conditional(s32[]{:T(128)} %convert_element_type.106, () %tuple.135, (pred[8,27]{1,0:T(8,128)(4,1)}, s32[8,189]{1,0:T(8,128)S(1)}, bf16[316,2016]{1,0:T(8,128)(2,1)S(1)}, s32[8,27]{1,0:T(8,128)}, bf16[512,2016]{1,0:T(8,128)(2,1)S(1)}) %tuple.136), branch_computations={%region_10.10_spmd, %region_11.12_spmd} | conditional | flops 2600168 | bytes 15764088 | solution.py:47
  981.6 17.6 %conditional.19 = (f32[8,2016]{1,0:T(8,128)}) conditional(s32[]{:T(128)} %convert_element_type.107, () %tuple.137, (pred[8,27]{1,0:T(8,128)(4,1)}, s32[8,189]{1,0:T(8,128)S(1)}, bf16[316,2016]{1,0:T(8,128)(2,1)S(1)}, s32[8,27]{1,0:T(8,128)}, bf16[512,2016]{1,0:T(8,128)(2,1)S(1)}) %tuple.138), branch_computations={%region_2.2_spmd, %region_3.4_spmd} | conditional | flops 2600168 | bytes 15764088 | solution.py:47
  999.9 17.7 %conditional.20 = (f32[8,2016]{1,0:T(8,128)}) conditional(s32[]{:T(128)} %convert_element_type.108, () %tuple.139, (pred[8,27]{1,0:T(8,128)(4,1)}, s32[8,189]{1,0:T(8,128)S(1)}, bf16[316,2016]{1,0:T(8,128)(2,1)S(1)}, s32[8,27]{1,0:T(8,128)}, bf16[512,2016]{1,0:T(8,128)(2,1)S(1)}) %tuple.140), branch_computations={%region_6.6_spmd, %region_7.8_spmd} | conditional | flops 2600168 | bytes 15764088 | solution.py:47
  1018.3 15.3 %conditional.14 = (f32[8,2016]{1,0:T(8,128)}) conditional(s32[]{:T(128)} %convert_element_type.102, () %tuple.127, (pred[8,27]{1,0:T(8,128)(4,1)}, s32[8,189]{1,0:T(8,128)S(1)}, bf16[316,2016]{1,0:T(8,128)(2,1)S(1)}, s32[8,27]{1,0:T(8,128)S(1)}, bf16[512,2016]{1,0:T(8,128)(2,1)S(1)}) %tuple.128), branch_computations={%region_26.26_spmd, %region_27.28_spmd} | conditional | flops 2600168 | bytes 15760604 | solution.py:47
  (856 shorter events, 966.6 us)
Async XLA Ops:
  0.6 3.0 copy-start.15
  0.6 3.0 copy-start.16
  5.2 7.0 copy-start.1
  6.2 6.0 collective-permute-start
  13.7 12.6 %copy-start.2 = (bf16[64,1008]{1,0:T(8,128)(2,1)}, bf16[64,1008]{1,0:T(8,128)(2,1)S(1)}, u32[]{:S(2)}) copy-start(bf16[64,1008]{1,0:T(8,128)(2,1)S(1)} %fusion.30) | copy-start | bytes 387076
  15.1 11.2 %collective-permute-start.1 = (bf16[64,2016]{1,0:T(8,128)(2,1)}, bf16[64,2016]{1,0:T(8,128)(2,1)S(1)}, u32[]{:S(2)}, u32[]{:S(2)}) collective-permute-start(bf16[64,2016]{1,0:T(8,128)(2,1)} %pad_maximum_fusion.3), channel_id=1, source_target_pairs={{25,0},{26,1},{27,2},{28,3},{29,4},{30,5},{31,6},{0,7},{1,8},{2,9}... | collective-permute-start | bytes 774152 | tf_op jit(solution)/shard_map/ppermute | solution.py:18
  16.9 15.5 %collective-permute-start.2 = (bf16[64,2016]{1,0:T(8,128)(2,1)}, bf16[64,2016]{1,0:T(8,128)(2,1)}, u32[]{:S(2)}, u32[]{:S(2)}) collective-permute-start(bf16[64,2016]{1,0:T(8,128)(2,1)} %pad_maximum_fusion.3), channel_id=1, source_target_pairs={{26,0},{27,1},{28,2},{29,3},{30,4},{31,5},{0,6},{1,7},{2,8},{3,9},... | collective-permute-start | bytes 774152 | tf_op jit(solution)/shard_map/ppermute | solution.py:18
  19.0 34.7 %copy-start = (bf16[316,2016]{1,0:T(8,128)(2,1)S(1)}, bf16[316,2016]{1,0:T(8,128)(2,1)}, u32[]{:S(2)}) copy-start(bf16[316,2016]{1,0:T(8,128)(2,1)} %param.29) | copy-start | bytes 3822340
  19.0 20.7 %collective-permute-start.3 = (bf16[64,2016]{1,0:T(8,128)(2,1)}, bf16[64,2016]{1,0:T(8,128)(2,1)S(1)}, u32[]{:S(2)}, u32[]{:S(2)}) collective-permute-start(bf16[64,2016]{1,0:T(8,128)(2,1)} %pad_maximum_fusion.3), channel_id=1, source_target_pairs={{27,0},{28,1},{29,2},{30,3},{31,4},{0,5},{1,6},{2,7},{3,8},{4,9},{... | collective-permute-start | bytes 774152 | tf_op jit(solution)/shard_map/ppermute | solution.py:18
  22.1 18.9 %collective-permute-start.4 = (bf16[64,2016]{1,0:T(8,128)(2,1)}, bf16[64,2016]{1,0:T(8,128)(2,1)S(1)}, u32[]{:S(2)}, u32[]{:S(2)}) collective-permute-start(bf16[64,2016]{1,0:T(8,128)(2,1)} %pad_maximum_fusion.3), channel_id=1, source_target_pairs={{28,0},{29,1},{30,2},{31,3},{0,4},{1,5},{2,6},{3,7},{4,8},{5,9},{6... | collective-permute-start | bytes 774152 | tf_op jit(solution)/shard_map/ppermute | solution.py:18
  24.2 27.1 %collective-permute-start.5 = (bf16[64,2016]{1,0:T(8,128)(2,1)}, bf16[64,2016]{1,0:T(8,128)(2,1)S(1)}, u32[]{:S(2)}, u32[]{:S(2)}) collective-permute-start(bf16[64,2016]{1,0:T(8,128)(2,1)} %pad_maximum_fusion.3), channel_id=1, source_target_pairs={{29,0},{30,1},{31,2},{0,3},{1,4},{2,5},{3,6},{4,7},{5,8},{6,9},{7,... | collective-permute-start | bytes 774152 | tf_op jit(solution)/shard_map/ppermute | solution.py:18
  27.0 26.6 %collective-permute-start.6 = (bf16[64,2016]{1,0:T(8,128)(2,1)}, bf16[64,2016]{1,0:T(8,128)(2,1)S(1)}, u32[]{:S(2)}, u32[]{:S(2)}) collective-permute-start(bf16[64,2016]{1,0:T(8,128)(2,1)} %pad_maximum_fusion.3), channel_id=1, source_target_pairs={{30,0},{31,1},{0,2},{1,3},{2,4},{3,5},{4,6},{5,7},{6,8},{7,9},{8,1... | collective-permute-start | bytes 774152 | tf_op jit(solution)/shard_map/ppermute | solution.py:18
  30.4 23.2 %copy-start.3 = (bf16[64,1008]{1,0:T(8,128)(2,1)S(1)}, bf16[64,1008]{1,0:T(8,128)(2,1)}, u32[]{:S(2)}) copy-start(bf16[64,1008]{1,0:T(8,128)(2,1)} %copy-done.2) | copy-start | bytes 387076
  32.4 21.2 %collective-permute-start.7 = (bf16[64,2016]{1,0:T(8,128)(2,1)}, bf16[64,2016]{1,0:T(8,128)(2,1)S(1)}, u32[]{:S(2)}, u32[]{:S(2)}) collective-permute-start(bf16[64,2016]{1,0:T(8,128)(2,1)} %pad_maximum_fusion.3), channel_id=1, source_target_pairs={{31,0},{0,1},{1,2},{2,3},{3,4},{4,5},{5,6},{6,7},{7,8},{8,9},{9,10... | collective-permute-start | bytes 774152 | tf_op jit(solution)/shard_map/ppermute | solution.py:18
  82.1 2.9 copy-start.14
  99.9 2.9 copy-start.13
  118.4 2.9 copy-start.12
  136.6 2.9 copy-start.11
  154.9 2.9 copy-start.10
  170.9 2.9 copy-start.9
  204.8 2.9 copy-start.14
  222.6 2.9 copy-start.13
  232.1 2.7 copy-start.5
  241.0 2.9 copy-start.12
  259.3 2.9 copy-start.11
  277.5 2.9 copy-start.10
  293.6 2.9 copy-start.9
  327.4 2.9 copy-start.14
  345.2 2.9 copy-start.13
  363.7 2.9 copy-start.12
  381.9 2.9 copy-start.11
  391.3 2.7 copy-start.7
  400.2 2.9 copy-start.10
  416.2 2.9 copy-start.9
  450.1 2.9 copy-start.14
  467.9 2.9 copy-start.13
  486.3 2.9 copy-start.12
  504.6 2.9 copy-start.11
  522.9 2.9 copy-start.10
  538.9 2.9 copy-start.9
  572.7 2.9 copy-start.14
  590.6 2.9 copy-start.13
  609.0 2.9 copy-start.12
  627.2 2.9 copy-start.11
  645.5 2.9 copy-start.10
  661.5 2.9 copy-start.9
  695.4 2.9 copy-start.14
  713.2 2.9 copy-start.13
  731.6 2.9 copy-start.12
  749.9 2.9 copy-start.11
  768.2 2.9 copy-start.10
  784.2 2.9 copy-start.9
  818.0 2.9 copy-start.14
  835.9 2.9 copy-start.13
  854.3 2.9 copy-start.12
  872.5 2.9 copy-start.11
  890.8 2.9 copy-start.10
  906.8 2.9 copy-start.9
  940.7 2.9 copy-start.14
  958.5 2.9 copy-start.13
  976.9 2.9 copy-start.12
  995.2 2.9 copy-start.11
  1013.5 2.9 copy-start.10
  1029.5 2.9 copy-start.9
  (31 other events, 82.4 us)
where the time goes:
time: 1050 us; the launch traced here: 1040 us
  local copies, waits for them, and re-layouts  614 us (58%)
  other arithmetic  337 us (32%)
  loops' own time  37.8 us (4%)
  waiting for transfers between devices  21.3 us (2%)
  starting transfers between devices  19.3 us (2%)
    sub x56, other arithmetic, compute(): coefficient[..., :half_width] * source_rows[..., :half_width]  160 us
    convert_element_type x56, local copies, waits for them, and re-layouts, compute(): coefficient = transfer[kind_piece].astype(jnp.float32)  152 us
    convert_element_type x56, local copies, waits for them, and re-layouts, compute(): source_table[jnp.clip(local_index, 0, row_count - 1)].astype(jnp.float32)  151 us
    gather x56, local copies, waits for them, and re-layouts, compute(): coefficient = transfer[kind_piece].astype(jnp.float32)  120 us
    gather x56, local copies, waits for them, and re-layouts, compute(): source_table[jnp.clip(local_index, 0, row_count - 1)].astype(jnp.float32)  120 us
    reduce_sum x56, other arithmetic, compute(): jnp.sum(jnp.where(live_mask[..., None], products, jnp.float32(0.0)), 1)  57.7 us
    select_n x56, other arithmetic, compute(): source_table[jnp.clip(local_index, 0, row_count - 1)].astype(jnp.float32)  48 us
    another operation x1, loops' own time, interact(): lax.map(one_block, (sources.reshape(block_count, 8, -1), kinds.reshape(bl...  35.6 us
  transfers between devices with their start and end apart: 8, of which 7 were waited for; matrix products, arithmetic and copies ran while one was open for 0% of the time, Pallas kernels for 0%

commit v1 on v0

v1 whole, which is shorter than its diff:
```python
import functools
import jax
import jax.numpy as jnp
from jax import lax
from jax.experimental import pallas as pl
from jax.experimental.pallas import tpu as pltpu
from jax.sharding import PartitionSpec as P

GBITS = 3
LANES = 128
CHUNK = 32
GROUP = 4


def passed_along(value, axis, steps):
    count = lax.axis_size(axis)
    first, last = (max(0, -steps), min(count, count - steps))
    return lax.ppermute(value, axis, [(source, source + steps) for source in range(first, last)])


def from_behind(block, axis, distance):
    devices = range(lax.axis_size(axis))
    route = [((i - distance) % len(devices), i) for i in devices]
    return lax.ppermute(block, axis, route)


def tiled(values, half_width, width):
    rows = values.shape[0]
    halves = values.reshape(rows, 2, half_width)
    halves = jnp.pad(halves, ((0, 0), (0, 0), (0, width - half_width)))
    return halves.reshape(rows, 2 * width // LANES, LANES)


def interact_kernel(fixed, chunk, half_width, count_ref, src_ref, kind_ref, table_ref, coef_ref, out_ref, sums):
    rows = table_ref.shape[1]
    half = rows // 2

    def some_slots(target, first, count, acc):
        re, im = acc
        for start in range(0, count, GROUP):
            ones, twos = [], []
            for slot in range(start, start + GROUP):
                source = table_ref[src_ref[target, first + slot]]
                kind = kind_ref[target, first + slot]
                ones.append(coef_ref[kind, :rows] * source)
                twos.append(coef_ref[kind, rows:] * source)
            while len(ones) > 1:
                ones = [ones[i] + ones[i + 1] for i in range(0, len(ones), 2)]
                twos = [twos[i] + twos[i + 1] for i in range(0, len(twos), 2)]
            one = ones[0].astype(jnp.float32)
            two = twos[0].astype(jnp.float32)
            re = re + (one[:half] + one[half:])
            im = im + (two[:half] + two[half:])
        return re, im

    def one_target(target, carry):
        zero = jnp.zeros((half, LANES), jnp.float32)
        acc = some_slots(target, 0, fixed, (zero, zero))
        more = count_ref[target]
        acc = lax.fori_loop(
            0, more, lambda i, acc: some_slots(target, fixed + i * chunk, chunk, acc), acc
        )
        sums[target, :half] = acc[0]
        sums[target, half:] = acc[1]
        return carry

    lax.fori_loop(0, src_ref.shape[0], one_target, 0)
    for part in range(2):
        pieces = [sums[:, part * half + i, :] for i in range(half)]
        whole = jnp.concatenate(pieces, 1)[:, :half_width]
        out_ref[:, part * half_width : (part + 1) * half_width] = whole.astype(out_ref.dtype)


def interact(table, sources, kinds, transfer, half_width):
    width = -(-half_width // LANES) * LANES
    targets, slots = sources.shape
    kinds_count = transfer.shape[0]
    fixed = -(-(slots // 2) // CHUNK) * CHUNK
    padded = fixed + -(-(slots - fixed) // CHUNK) * CHUNK
    live = sources >= 0
    tail = ((0, 0), (0, padded - slots))
    src = jnp.pad(jnp.where(live, sources, 0), tail)
    kind = jnp.pad(jnp.where(live, kinds, kinds_count), tail, constant_values=kinds_count)
    lengths = jnp.sum(live.astype(jnp.int32), 1)
    more = jnp.maximum(lengths - fixed + CHUNK - 1, 0) // CHUNK
    real, imag = transfer[:, :half_width], transfer[:, half_width:]
    ones = tiled(jnp.concatenate([real, -imag], 1), half_width, width)
    twos = tiled(jnp.concatenate([imag, real], 1), half_width, width)
    coef = jnp.pad(jnp.concatenate([ones, twos], 1), ((0, 1), (0, 0), (0, 0)))
    smem = pl.BlockSpec(memory_space=pltpu.SMEM)
    vmem = pl.BlockSpec(memory_space=pltpu.VMEM)
    return pl.pallas_call(
        functools.partial(interact_kernel, fixed, CHUNK, half_width),
        out_shape=jax.ShapeDtypeStruct((targets, 2 * half_width), jnp.bfloat16),
        in_specs=[smem, smem, smem, vmem, vmem],
        out_specs=vmem,
        scratch_shapes=[pltpu.VMEM((targets, table.shape[1], LANES), jnp.float32)],
        compiler_params=pltpu.CompilerParams(vmem_limit_bytes=24 * 2**20),
        name="interact",
    )(more, src, kind, table, coef)


def shards(
    leaf_spectra, leaf_keys, parent_keys, child_phase, coarsen, transfer, vlist_src, vlist_type
):
    half_width = child_phase.shape[1]
    child_code = leaf_keys % 8
    parent_of = leaf_keys // 8
    phase_table = jnp.concatenate([jnp.cos(child_phase), jnp.sin(child_phase)], 1)
    picker = (child_code[:, None] == jnp.arange(8, dtype=jnp.int32)[None, :]).astype(jnp.float32)
    factors = jnp.dot(picker, phase_table, precision=lax.Precision.HIGHEST)
    cosine = factors[:, :half_width]
    sine_part = factors[:, half_width:]
    spectra = leaf_spectra.astype(jnp.float32)
    real_in = spectra[:, :half_width]
    imag_in = spectra[:, half_width:]
    twisted = jnp.concatenate(
        [real_in * cosine - imag_in * sine_part, real_in * sine_part + imag_in * cosine], 1
    )
    membership = (parent_of[:, None] == parent_keys[None, :]).astype(jnp.float32)
    gathered = jnp.einsum("lp,lc->pc", membership, twisted, precision=lax.Precision.HIGHEST)
    tail_mask = (parent_of < parent_keys[0]).astype(jnp.float32)
    tail_sum = jnp.dot(tail_mask, twisted, precision=lax.Precision.HIGHEST)
    incoming = passed_along(tail_sum, "oct", -1)
    gathered = jnp.concatenate([gathered[:-1], gathered[-1:] + incoming[None, :]], 0)
    gathered_b = gathered.astype(jnp.bfloat16)
    real_b = gathered_b[:, :half_width]
    imag_b = gathered_b[:, half_width:]
    real_out = jnp.dot(real_b, coarsen[0], preferred_element_type=jnp.float32) - jnp.dot(
        imag_b, coarsen[1], preferred_element_type=jnp.float32
    )
    imag_out = jnp.dot(real_b, coarsen[1], preferred_element_type=jnp.float32) + jnp.dot(
        imag_b, coarsen[0], preferred_element_type=jnp.float32
    )
    upward = jnp.concatenate([real_out, imag_out], 1).astype(jnp.bfloat16)
    width = -(-half_width // LANES) * LANES
    own = tiled(upward, half_width, width)
    window_count = 2**GBITS
    blocks = [own]
    for distance in range(1, window_count):
        received = from_behind(own, "oct", distance)
        blocks = [received] + blocks
    table = jnp.concatenate(blocks, 0)
    local_field = interact(table, vlist_src, vlist_type, transfer, half_width)
    return (upward, local_field)


def solution(mesh):
    return jax.shard_map(
        shards,
        mesh=mesh,
        in_specs=(
            P("oct", None),
            P("oct"),
            P("oct"),
            P(),
            P(),
            P(),
            P("oct", None),
            P("oct", None),
        ),
        out_specs=(P("oct", None), P("oct", None)),
        check_vma=False,
    )
```

time: 1050 us -> 115 us (0.11)
  the two profiles are of different devices: /device:TPU:1 before, /device:TPU:0 now
where the time goes in v1:
time: 115 us
  Pallas kernels  42 us (37%)
  waiting for transfers between devices  32 us (28%)
  starting transfers between devices  14.6 us (13%)
  local copies, waits for them, and re-layouts  12.9 us (11%)
  other arithmetic  6.79 us (6%)
  matrix products  5.35 us (5%)
    pallas_call x1, Pallas kernels, interact(): pl.pallas_call(functools.partial(interact_kernel, fixed, CHUNK, half_widt...  42 us
    ppermute x7, waiting for transfers between devices, from_behind(): return lax.ppermute(block, axis, route)  32 us
    ppermute x7, starting transfers between devices, from_behind(): return lax.ppermute(block, axis, route)  13.1 us
    reshape x2, local copies, waits for them, and re-layouts, tiled(): halves = values.reshape(rows, 2, half_width)  3.7 us
    pad x3, local copies, waits for them, and re-layouts, tiled(): halves = jnp.pad(halves, ((0, 0), (0, 0), (0, width - half_width)))  3.62 us
    reshape x3, local copies, waits for them, and re-layouts, tiled(): return halves.reshape(rows, 2 * width // LANES, LANES)  3.59 us
  transfers between devices with their start and end apart: 8, of which 6 were waited for; matrix products, arithmetic and copies ran while one was open for 14% of the time, Pallas kernels for 0%

profile of v1, /device:TPU:0, one launch (start us, length us, event | category | flops | bytes accessed | tf_op | source)
XLA Modules:
  0.0 114.5 jit_solution(7365102390677974148)
XLA Ops:
  0.6 0.0 copy-start.4
  0.6 0.0 copy-start.5
  0.7 0.9 fusion.45
  1.6 0.7 and_select_fusion.1
  2.2 1.4 %convert_element_type.11 = f32[256,2016]{0,1:T(8,128)S(1)} convert(bf16[256,2016]{0,1:T(8,128)(2,1)} %param.8) | non-fusion elementwise | flops 516096 | bytes 3096576 | tf_op jit(solution)/shard_map/convert_element_type | solution.py:114
  3.6 0.0 copy-done.4
  3.6 0.0 copy-done.5
  3.7 1.2 %fusion.30 = f32[256,2016]{0,1:T(8,128)S(1)} fusion(f32[8,1008]{1,0:T(8,128)S(1)} %get-tuple-element.15, f32[8,1008]{1,0:T(8,128)S(1)} %get-tuple-element.14, s32[256]{0:T(256)S(1)} %and_select_fusion.1), kind=kOutput, calls=%fused_computation.35 | convolution fusion | flops 49563392 | bytes 2129920 | tf_op jit(solution)/shard_map/dot_general | solution.py:111
  4.9 0.3 multiply_subtract_fusion
  5.2 0.0 copy-start
  5.2 1.0 fusion.15
  6.2 1.5 %collective-permute-start = (f32[2016]{0:T(1024)S(1)}, f32[2016]{0:T(1024)S(1)}, u32[]{:S(2)}, u32[]{:S(2)}) collective-permute-start(f32[2016]{0:T(1024)S(1)} %bitcast.27), channel_id=1, source_target_pairs={{1,0},{2,1},{3,2},{4,3},{5,4},{6,5},{7,6},{8,7},{9,8},{10,9},{11,1... | collective-permute-start | bytes 24200 | tf_op jit(solution)/shard_map/ppermute | solution.py:18
  7.7 1.1 fusion.16
  8.8 0.0 copy-done
  8.9 0.3 slice_negate_fusion
  9.1 0.9 pad_maximum_fusion.3
  10.0 2.4 %reshape.28 = bf16[316,2,1008]{2,1,0:T(2,128)(2,1)} reshape(bf16[316,2016]{1,0:T(8,128)(2,1)S(1)} %get-tuple-element.9) | data formatting | bytes 2548224 | tf_op jit(solution)/shard_map/reshape | solution.py:29
  12.4 2.4 %pad.25 = bf16[316,2,1024]{2,1,0:T(2,128)(2,1)S(1)} pad(bf16[316,2,1008]{2,1,0:T(2,128)(2,1)} %reshape.28, bf16[]{:T(256)} %constant.57.clone.1), padding=0_0x0_0x0_16 | pad | bytes 2568450 | tf_op jit(solution)/shard_map/jit(_pad)/pad | solution.py:30
  14.8 1.7 %reshape.29 = bf16[316,16,128]{2,1,0:T(8,128)(2,1)} reshape(bf16[316,2,1024]{2,1,0:T(2,128)(2,1)S(1)} %pad.25) | data formatting | bytes 2588672 | tf_op jit(solution)/shard_map/reshape | solution.py:31
  16.5 1.3 %reshape.30 = bf16[316,2,1008]{2,1,0:T(2,128)(2,1)S(1)} reshape(bf16[316,2016]{1,0:T(8,128)(2,1)S(1)} %get-tuple-element.10) | data formatting | bytes 2548224 | tf_op jit(solution)/shard_map/reshape | solution.py:29
  17.8 1.0 pad.26
  18.8 1.7 %reshape.31 = bf16[316,16,128]{2,1,0:T(8,128)(2,1)} reshape(bf16[316,2,1024]{2,1,0:T(2,128)(2,1)S(1)} %pad.26) | data formatting | bytes 2588672 | tf_op jit(solution)/shard_map/reshape | solution.py:31
  20.6 0.0 copy-start.2
  20.6 0.0 copy-start.3
  20.6 0.0 copy-start.1
  20.6 2.3 %fusion.2.coef_ref = bf16[317,32,128]{2,1,0:T(8,128)(2,1)S(1)} fusion(bf16[316,16,128]{2,1,0:T(8,128)(2,1)} %reshape.31, bf16[316,16,128]{2,1,0:T(8,128)(2,1)} %reshape.29), kind=kLoop, calls=%fused_computation.3 | loop fusion | flops 9089024 | bytes 5185536 | tf_op jit(solution)/shard_map/concatenate | solution.py:89
  22.9 0.0 copy-done.2
  22.9 0.0 copy-done.3
  22.9 0.1 broadcast_select_fusion
  23.0 0.0 collective-permute-done
  23.1 0.5 copy-done.1
  23.6 0.5 fusion.5
  24.1 0.5 fusion.3
  24.6 0.5 fusion.26
  25.1 0.5 fusion.23
  25.6 0.3 copy.11
  25.9 0.2 pad.24.clone
  26.1 0.2 reshape.27
  26.3 4.7 %collective-permute-start.1 = (bf16[64,16,128]{2,1,0:T(8,128)(2,1)S(1)}, bf16[64,16,128]{2,1,0:T(8,128)(2,1)S(1)}, u32[]{:S(2)}, u32[]{:S(2)}) collective-permute-start(bf16[64,16,128]{2,1,0:T(8,128)(2,1)S(1)} %reshape.27), channel_id=1, source_target_pairs={{25,0},{26,1},{27,2},{28,3},{29,4},{30,5},{31,6},{0,7},{1,8},{2,9}... | collective-permute-start | bytes 786440 | tf_op jit(solution)/shard_map/ppermute | solution.py:24
  31.0 1.6 %collective-permute-start.2 = (bf16[64,16,128]{2,1,0:T(8,128)(2,1)S(1)}, bf16[64,16,128]{2,1,0:T(8,128)(2,1)S(1)}, u32[]{:S(2)}, u32[]{:S(2)}) collective-permute-start(bf16[64,16,128]{2,1,0:T(8,128)(2,1)S(1)} %reshape.27), channel_id=1, source_target_pairs={{26,0},{27,1},{28,2},{29,3},{30,4},{31,5},{0,6},{1,7},{2,8},{3,9},... | collective-permute-start | bytes 786440 | tf_op jit(solution)/shard_map/ppermute | solution.py:24
  32.6 0.9 collective-permute-start.3
  33.5 1.5 %collective-permute-start.4 = (bf16[64,16,128]{2,1,0:T(8,128)(2,1)S(1)}, bf16[64,16,128]{2,1,0:T(8,128)(2,1)S(1)}, u32[]{:S(2)}, u32[]{:S(2)}) collective-permute-start(bf16[64,16,128]{2,1,0:T(8,128)(2,1)S(1)} %reshape.27), channel_id=1, source_target_pairs={{28,0},{29,1},{30,2},{31,3},{0,4},{1,5},{2,6},{3,7},{4,8},{5,9},{6... | collective-permute-start | bytes 786440 | tf_op jit(solution)/shard_map/ppermute | solution.py:24
  35.0 1.6 %collective-permute-start.5 = (bf16[64,16,128]{2,1,0:T(8,128)(2,1)S(1)}, bf16[64,16,128]{2,1,0:T(8,128)(2,1)S(1)}, u32[]{:S(2)}, u32[]{:S(2)}) collective-permute-start(bf16[64,16,128]{2,1,0:T(8,128)(2,1)S(1)} %reshape.27), channel_id=1, source_target_pairs={{29,0},{30,1},{31,2},{0,3},{1,4},{2,5},{3,6},{4,7},{5,8},{6,9},{7,... | collective-permute-start | bytes 786440 | tf_op jit(solution)/shard_map/ppermute | solution.py:24
  36.6 0.8 pad_maximum_fusion.5
  37.4 0.0 collective-permute-done.1
  37.4 2.9 %collective-permute-start.6 = (bf16[64,16,128]{2,1,0:T(8,128)(2,1)S(1)}, bf16[64,16,128]{2,1,0:T(8,128)(2,1)S(1)}, u32[]{:S(2)}, u32[]{:S(2)}) collective-permute-start(bf16[64,16,128]{2,1,0:T(8,128)(2,1)S(1)} %reshape.27), channel_id=1, source_target_pairs={{30,0},{31,1},{0,2},{1,3},{2,4},{3,5},{4,6},{5,7},{6,8},{7,9},{8,1... | collective-permute-start | bytes 786440 | tf_op jit(solution)/shard_map/ppermute | solution.py:24
  40.3 5.5 %collective-permute-done.2 = bf16[64,16,128]{2,1,0:T(8,128)(2,1)S(1)} collective-permute-done((bf16[64,16,128]{2,1,0:T(8,128)(2,1)S(1)}, bf16[64,16,128]{2,1,0:T(8,128)(2,1)S(1)}, u32[]{:S(2)}, u32[]{:S(2)}) %collective-permute-start.2) | collective-permute-done | bytes 262176 | tf_op jit(solution)/shard_map/ppermute | solution.py:24
  45.8 0.0 collective-permute-start.7
  45.9 2.6 %collective-permute-done.3 = bf16[64,16,128]{2,1,0:T(8,128)(2,1)S(1)} collective-permute-done((bf16[64,16,128]{2,1,0:T(8,128)(2,1)S(1)}, bf16[64,16,128]{2,1,0:T(8,128)(2,1)S(1)}, u32[]{:S(2)}, u32[]{:S(2)}) %collective-permute-start.3) | collective-permute-done | bytes 262176 | tf_op jit(solution)/shard_map/ppermute | solution.py:24
  48.5 9.7 %collective-permute-done.4 = bf16[64,16,128]{2,1,0:T(8,128)(2,1)S(1)} collective-permute-done((bf16[64,16,128]{2,1,0:T(8,128)(2,1)S(1)}, bf16[64,16,128]{2,1,0:T(8,128)(2,1)S(1)}, u32[]{:S(2)}, u32[]{:S(2)}) %collective-permute-start.4) | collective-permute-done | bytes 262176 | tf_op jit(solution)/shard_map/ppermute | solution.py:24
  58.2 3.0 %collective-permute-done.5 = bf16[64,16,128]{2,1,0:T(8,128)(2,1)S(1)} collective-permute-done((bf16[64,16,128]{2,1,0:T(8,128)(2,1)S(1)}, bf16[64,16,128]{2,1,0:T(8,128)(2,1)S(1)}, u32[]{:S(2)}, u32[]{:S(2)}) %collective-permute-start.5) | collective-permute-done | bytes 262176 | tf_op jit(solution)/shard_map/ppermute | solution.py:24
  61.2 8.9 %collective-permute-done.6 = bf16[64,16,128]{2,1,0:T(8,128)(2,1)S(1)} collective-permute-done((bf16[64,16,128]{2,1,0:T(8,128)(2,1)S(1)}, bf16[64,16,128]{2,1,0:T(8,128)(2,1)S(1)}, u32[]{:S(2)}, u32[]{:S(2)}) %collective-permute-start.6) | collective-permute-done | bytes 262176 | tf_op jit(solution)/shard_map/ppermute | solution.py:24
  70.1 2.4 %collective-permute-done.7 = bf16[64,16,128]{2,1,0:T(8,128)(2,1)S(1)} collective-permute-done((bf16[64,16,128]{2,1,0:T(8,128)(2,1)S(1)}, bf16[64,16,128]{2,1,0:T(8,128)(2,1)S(1)}, u32[]{:S(2)}, u32[]{:S(2)}) %collective-permute-start.7) | collective-permute-done | bytes 262176 | tf_op jit(solution)/shard_map/ppermute | solution.py:24
  72.6 42.0 %interact.1 = bf16[64,2016]{1,0:T(8,128)(2,1)} custom-call(s32[64]{0:T(128)S(1)} %and_select_fusion.count_ref, s32[64,192]{1,0:T(8,128)S(1)} %pad.22.src_ref, s32[64,192]{1,0:T(8,128)S(1)} %pad.23.kind_ref, bf16[512,16,128]{2,1,0:T(8,128)(2,1)S(1)} %constant_dynamic-update-slice_fusion.table_ref, bf16[317,32,128]{2,1,0:T(8,128)(2,1)S(1)} %fusion.2.coef_ref), custom_call_target="tpu_custom_call" | custom-call | tf_op jit(solution)/shard_map/interact/pallas_call | solution.py:92
  (16 shorter events, 0.4 us)
Async XLA Ops:
  0.6 3.0 %copy-start.4 = (s32[256]{0:T(256)S(1)}, s32[256]{0:T(256)}, u32[]{:S(2)}) copy-start(s32[256]{0:T(256)} %param.9) | copy-start | bytes 3076
  0.6 3.0 %copy-start.5 = (s32[64]{0:T(128)S(1)}, s32[64]{0:T(128)}, u32[]{:S(2)}) copy-start(s32[64]{0:T(128)} %param.10) | copy-start | bytes 772
  5.2 3.7 %copy-start = (bf16[316,2016]{1,0:T(8,128)(2,1)S(1)}, bf16[316,2016]{1,0:T(8,128)(2,1)}, u32[]{:S(2)}) copy-start(bf16[316,2016]{1,0:T(8,128)(2,1)} %param.13) | copy-start | bytes 3822340
  6.2 16.8 %collective-permute-start = (f32[2016]{0:T(1024)S(1)}, f32[2016]{0:T(1024)S(1)}, u32[]{:S(2)}, u32[]{:S(2)}) collective-permute-start(f32[2016]{0:T(1024)S(1)} %bitcast.27), channel_id=1, source_target_pairs={{1,0},{2,1},{3,2},{4,3},{5,4},{6,5},{7,6},{8,7},{9,8},{10,9},{11,1... | collective-permute-start | bytes 24200 | tf_op jit(solution)/shard_map/ppermute | solution.py:18
  20.6 2.3 %copy-start.2 = (s32[64,189]{1,0:T(8,128)S(1)}, s32[64,189]{1,0:T(8,128)}, u32[]{:S(2)}) copy-start(s32[64,189]{1,0:T(8,128)} %param.15) | copy-start | bytes 145156
  20.6 2.3 %copy-start.3 = (s32[64,189]{1,0:T(8,128)S(1)}, s32[64,189]{1,0:T(8,128)}, u32[]{:S(2)}) copy-start(s32[64,189]{1,0:T(8,128)} %param.14) | copy-start | bytes 145156
  20.6 3.0 %copy-start.1 = (bf16[2,1008,1008]{2,1,0:T(8,128)(2,1)S(1)}, bf16[2,1008,1008]{2,1,0:T(8,128)(2,1)}, u32[]{:S(2)}) copy-start(bf16[2,1008,1008]{2,1,0:T(8,128)(2,1)} %param.12) | copy-start | bytes 12192772
  26.3 11.1 %collective-permute-start.1 = (bf16[64,16,128]{2,1,0:T(8,128)(2,1)S(1)}, bf16[64,16,128]{2,1,0:T(8,128)(2,1)S(1)}, u32[]{:S(2)}, u32[]{:S(2)}) collective-permute-start(bf16[64,16,128]{2,1,0:T(8,128)(2,1)S(1)} %reshape.27), channel_id=1, source_target_pairs={{25,0},{26,1},{27,2},{28,3},{29,4},{30,5},{31,6},{0,7},{1,8},{2,9}... | collective-permute-start | bytes 786440 | tf_op jit(solution)/shard_map/ppermute | solution.py:24
  31.0 14.8 %collective-permute-start.2 = (bf16[64,16,128]{2,1,0:T(8,128)(2,1)S(1)}, bf16[64,16,128]{2,1,0:T(8,128)(2,1)S(1)}, u32[]{:S(2)}, u32[]{:S(2)}) collective-permute-start(bf16[64,16,128]{2,1,0:T(8,128)(2,1)S(1)} %reshape.27), channel_id=1, source_target_pairs={{26,0},{27,1},{28,2},{29,3},{30,4},{31,5},{0,6},{1,7},{2,8},{3,9},... | collective-permute-start | bytes 786440 | tf_op jit(solution)/shard_map/ppermute | solution.py:24
  32.6 15.8 %collective-permute-start.3 = (bf16[64,16,128]{2,1,0:T(8,128)(2,1)S(1)}, bf16[64,16,128]{2,1,0:T(8,128)(2,1)S(1)}, u32[]{:S(2)}, u32[]{:S(2)}) collective-permute-start(bf16[64,16,128]{2,1,0:T(8,128)(2,1)S(1)} %reshape.27), channel_id=1, source_target_pairs={{27,0},{28,1},{29,2},{30,3},{31,4},{0,5},{1,6},{2,7},{3,8},{4,9},{... | collective-permute-start | bytes 786440 | tf_op jit(solution)/shard_map/ppermute | solution.py:24
  33.5 24.7 %collective-permute-start.4 = (bf16[64,16,128]{2,1,0:T(8,128)(2,1)S(1)}, bf16[64,16,128]{2,1,0:T(8,128)(2,1)S(1)}, u32[]{:S(2)}, u32[]{:S(2)}) collective-permute-start(bf16[64,16,128]{2,1,0:T(8,128)(2,1)S(1)} %reshape.27), channel_id=1, source_target_pairs={{28,0},{29,1},{30,2},{31,3},{0,4},{1,5},{2,6},{3,7},{4,8},{5,9},{6... | collective-permute-start | bytes 786440 | tf_op jit(solution)/shard_map/ppermute | solution.py:24
  35.0 26.2 %collective-permute-start.5 = (bf16[64,16,128]{2,1,0:T(8,128)(2,1)S(1)}, bf16[64,16,128]{2,1,0:T(8,128)(2,1)S(1)}, u32[]{:S(2)}, u32[]{:S(2)}) collective-permute-start(bf16[64,16,128]{2,1,0:T(8,128)(2,1)S(1)} %reshape.27), channel_id=1, source_target_pairs={{29,0},{30,1},{31,2},{0,3},{1,4},{2,5},{3,6},{4,7},{5,8},{6,9},{7,... | collective-permute-start | bytes 786440 | tf_op jit(solution)/shard_map/ppermute | solution.py:24
  37.4 32.7 %collective-permute-start.6 = (bf16[64,16,128]{2,1,0:T(8,128)(2,1)S(1)}, bf16[64,16,128]{2,1,0:T(8,128)(2,1)S(1)}, u32[]{:S(2)}, u32[]{:S(2)}) collective-permute-start(bf16[64,16,128]{2,1,0:T(8,128)(2,1)S(1)} %reshape.27), channel_id=1, source_target_pairs={{30,0},{31,1},{0,2},{1,3},{2,4},{3,5},{4,6},{5,7},{6,8},{7,9},{8,1... | collective-permute-start | bytes 786440 | tf_op jit(solution)/shard_map/ppermute | solution.py:24
  45.8 26.7 %collective-permute-start.7 = (bf16[64,16,128]{2,1,0:T(8,128)(2,1)S(1)}, bf16[64,16,128]{2,1,0:T(8,128)(2,1)S(1)}, u32[]{:S(2)}, u32[]{:S(2)}) collective-permute-start(bf16[64,16,128]{2,1,0:T(8,128)(2,1)S(1)} %reshape.27), channel_id=1, source_target_pairs={{31,0},{0,1},{1,2},{2,3},{3,4},{4,5},{5,6},{6,7},{7,8},{8,9},{9,10... | collective-permute-start | bytes 786440 | tf_op jit(solution)/shard_map/ppermute | solution.py:24

commit v2 on v1

--- a/solution.py
+++ b/solution.py
@@ -9,19 +9,13 @@
 GBITS = 3
 LANES = 128
 CHUNK = 32
-GROUP = 4
+PARTS = 2
 
 
 def passed_along(value, axis, steps):
     count = lax.axis_size(axis)
     first, last = (max(0, -steps), min(count, count - steps))
     return lax.ppermute(value, axis, [(source, source + steps) for source in range(first, last)])
-
-
-def from_behind(block, axis, distance):
-    devices = range(lax.axis_size(axis))
-    route = [((i - distance) % len(devices), i) for i in devices]
-    return lax.ppermute(block, axis, route)
 
 
 def tiled(values, half_width, width):
@@ -31,26 +25,157 @@
     return halves.reshape(rows, 2 * width // LANES, LANES)
 
 
-def interact_kernel(fixed, chunk, half_width, count_ref, src_ref, kind_ref, table_ref, coef_ref, out_ref, sums):
-    rows = table_ref.shape[1]
+def exchange_kernel(axis, count, group, own_ref, window_ref, prev_ref, *sems):
+    z_send, z_recv, far_send, far_recv, near_send, near_recv, pass_send, pass_recv, own_sem = sems
+    me = lax.axis_index(axis)
+    r = lax.rem(me, group)
+    base = me - r
+    after = lax.rem(me + group, count)
+    before = lax.rem(me + count - group, count)
+    twin = me + 1 - 2 * lax.rem(r, 2)
+    steps = range(2, group, 2)
+    piece = own_ref.shape[0] // PARTS
+
+    barrier = pltpu.get_barrier_semaphore()
+    greeted = [after, before, twin] + [base + lax.rem(r + step, group) for step in steps]
+    for device in greeted:
+        pl.semaphore_signal(barrier, inc=1, device_id={axis: device}, device_id_type=pl.DeviceIdType.MESH)
+    pl.semaphore_wait(barrier, len(greeted))
+
+    def copy(source, target, send, recv, device):
+        return pltpu.make_async_remote_copy(
+            src_ref=source, dst_ref=target, send_sem=send, recv_sem=recv,
+            device_id={axis: device}, device_id_type=pl.DeviceIdType.MESH,
+        )
+
+    def rows_of(part):
+        return pl.ds(part * piece, piece)
+
+    def along(part):
+        return copy(own_ref.at[rows_of(part)], prev_ref.at[rows_of(part)], z_send.at[part], z_recv.at[part], after)
+
+    def far(block, index, part):
+        peer = base + lax.rem(r + steps[index], group)
+        return copy(
+            block.at[rows_of(part)], window_ref.at[r, rows_of(part)],
+            far_send.at[index, part], far_recv.at[index, part], peer,
+        )
+
+    def near(block, part):
+        return copy(
+            block.at[rows_of(part)], window_ref.at[r, rows_of(part)], near_send.at[part], near_recv.at[part], twin
+        )
+
+    def onward(index, part):
+        slot = lax.rem(r + group - steps[index], group)
+        here = window_ref.at[slot, rows_of(part)]
+        return copy(here, here, pass_send.at[index, part], pass_recv.at[index, part], twin)
+
+    parts = range(PARTS)
+    indices = range(len(steps))
+    for part in parts:
+        along(part).start()
+    for part in parts:
+        for index in indices:
+            @pl.when(r + steps[index] < group)
+            def _():
+                far(own_ref, index, part).start()
+    @pl.when(lax.rem(r, 2) == 0)
+    def _():
+        for part in parts:
+            near(own_ref, part).start()
+    own_copy = pltpu.make_async_copy(own_ref, window_ref.at[r], own_sem)
+    own_copy.start()
+    for part in parts:
+        along(part).wait_recv()
+        for index in indices:
+            @pl.when(r + steps[index] >= group)
+            def _():
+                far(prev_ref, index, part).start()
+        @pl.when(lax.rem(r, 2) == 1)
+        def _():
+            near(prev_ref, part).start()
+    for index in indices:
+        for part in parts:
+            far(own_ref, index, part).wait_recv()
+            onward(index, part).start()
+    for part in parts:
+        near(own_ref, part).wait_recv()
+        for index in indices:
+            onward(index, part).wait_recv()
+    for part in parts:
+        along(part).wait_send()
+        near(own_ref, part).wait_send()
+        for index in indices:
+            far(own_ref, index, part).wait_send()
+            onward(index, part).wait_send()
+    own_copy.wait()
+
+
+def exchange(own, axis, group):
+    others = group // 2 - 1
+    dma = pltpu.SemaphoreType.DMA
+    anywhere = pl.BlockSpec(memory_space=pl.ANY)
+    return pl.pallas_call(
+        functools.partial(exchange_kernel, axis, lax.axis_size(axis), group),
+        out_shape=[
+            jax.ShapeDtypeStruct((group,) + own.shape, own.dtype),
+            jax.ShapeDtypeStruct(own.shape, own.dtype),
+        ],
+        in_specs=[anywhere],
+        out_specs=[anywhere, anywhere],
+        scratch_shapes=[
+            dma((PARTS,)), dma((PARTS,)),
+            dma((others, PARTS)), dma((others, PARTS)),
+            dma((PARTS,)), dma((PARTS,)),
+            dma((others, PARTS)), dma((others, PARTS)),
+            dma,
+        ],
+        compiler_params=pltpu.CompilerParams(collective_id=0, has_side_effects=True),
+        name="exchange",
+    )(own)[0]
+
+
+def interact_kernel(
+    fixed, chunk, half_width, count_ref, src_ref, kind_ref, window_ref, transfer_ref, out_ref, table, coef, sums
+):
+    rows = table.shape[1]
     half = rows // 2
+    kinds = transfer_ref.shape[0]
+    step = 16
+
+    def widen(i, carry):
+        part = pl.ds(pl.multiple_of(i * step, step), step)
+        table[part] = window_ref[part].astype(jnp.float32)
+        return carry
+
+    lax.fori_loop(0, table.shape[0] // step, widen, 0)
+
+    def lay_out(start, count):
+        block = transfer_ref[pl.ds(start, count), :].astype(jnp.float32)
+        for part in range(2):
+            whole = block[:, part * half_width : (part + 1) * half_width]
+            whole = jnp.concatenate([whole, jnp.zeros((count, half * LANES - half_width), jnp.float32)], 1)
+            for i in range(half):
+                coef[pl.ds(start, count), part * half + i, :] = whole[:, i * LANES : (i + 1) * LANES]
+
+    def lay_out_step(i, carry):
+        lay_out(pl.multiple_of(i * step, step), step)
+        return carry
+
+    even = kinds // step
+    lax.fori_loop(0, even, lay_out_step, 0)
+    if kinds % step:
+        lay_out(even * step, kinds % step)
+    coef[kinds] = jnp.zeros(coef.shape[1:], jnp.float32)
 
     def some_slots(target, first, count, acc):
         re, im = acc
-        for start in range(0, count, GROUP):
-            ones, twos = [], []
-            for slot in range(start, start + GROUP):
-                source = table_ref[src_ref[target, first + slot]]
-                kind = kind_ref[target, first + slot]
-                ones.append(coef_ref[kind, :rows] * source)
-                twos.append(coef_ref[kind, rows:] * source)
-            while len(ones) > 1:
-                ones = [ones[i] + ones[i + 1] for i in range(0, len(ones), 2)]
-                twos = [twos[i] + twos[i + 1] for i in range(0, len(twos), 2)]
-            one = ones[0].astype(jnp.float32)
-            two = twos[0].astype(jnp.float32)
-            re = re + (one[:half] + one[half:])
-            im = im + (two[:half] + two[half:])
+        for slot in range(count):
+            source = table[src_ref[target, first + slot]]
+            factor = coef[kind_ref[target, first + slot]]
+            re = re + (factor[:half] * source[:half] - factor[half:] * source[half:])
+            im = im + (factor[:half] * source[half:] + factor[half:] * source[:half])
         return re, im
 
     def one_target(target, carry):
@@ -71,8 +196,8 @@
         out_ref[:, part * half_width : (part + 1) * half_width] = whole.astype(out_ref.dtype)
 
 
-def interact(table, sources, kinds, transfer, half_width):
-    width = -(-half_width // LANES) * LANES
+def interact(window, sources, kinds, transfer, half_width):
+    rows = window.shape[1]
     targets, slots = sources.shape
     kinds_count = transfer.shape[0]
     fixed = -(-(slots // 2) // CHUNK) * CHUNK
@@ -83,10 +208,6 @@
     kind = jnp.pad(jnp.where(live, kinds, kinds_count), tail, constant_values=kinds_count)
     lengths = jnp.sum(live.astype(jnp.int32), 1)
     more = jnp.maximum(lengths - fixed + CHUNK - 1, 0) // CHUNK
-    real, imag = transfer[:, :half_width], transfer[:, half_width:]
-    ones = tiled(jnp.concatenate([real, -imag], 1), half_width, width)
-    twos = tiled(jnp.concatenate([imag, real], 1), half_width, width)
-    coef = jnp.pad(jnp.concatenate([ones, twos], 1), ((0, 1), (0, 0), (0, 0)))
     smem = pl.BlockSpec(memory_space=pltpu.SMEM)
     vmem = pl.BlockSpec(memory_space=pltpu.VMEM)
     return pl.pallas_call(
@@ -94,10 +215,14 @@
         out_shape=jax.ShapeDtypeStruct((targets, 2 * half_width), jnp.bfloat16),
         in_specs=[smem, smem, smem, vmem, vmem],
         out_specs=vmem,
-        scratch_shapes=[pltpu.VMEM((targets, table.shape[1], LANES), jnp.float32)],
-        compiler_params=pltpu.CompilerParams(vmem_limit_bytes=24 * 2**20),
+        scratch_shapes=[
+            pltpu.VMEM(window.shape, jnp.float32),
+            pltpu.VMEM((kinds_count + 1, rows, LANES), jnp.float32),
+            pltpu.VMEM((targets, rows, LANES), jnp.float32),
+        ],
+        compiler_params=pltpu.CompilerParams(vmem_limit_bytes=32 * 2**20),
         name="interact",
-    )(more, src, kind, table, coef)
+    )(more, src, kind, window, transfer)
 
 
 def shards(
@@ -135,13 +260,13 @@
     upward = jnp.concatenate([real_out, imag_out], 1).astype(jnp.bfloat16)
     width = -(-half_width // LANES) * LANES
     own = tiled(upward, half_width, width)
-    window_count = 2**GBITS
-    blocks = [own]
-    for distance in range(1, window_count):
-        received = from_behind(own, "oct", distance)
-        blocks = [received] + blocks
-    table = jnp.concatenate(blocks, 0)
-    local_field = interact(table, vlist_src, vlist_type, transfer, half_width)
+    group = 2**GBITS
+    rows = own.shape[0]
+    window = exchange(own, "oct", group).reshape((group * rows,) + own.shape[1:])
+    rank = lax.rem(lax.axis_index("oct"), group)
+    slot = (vlist_src // rows + rank + 1) % group
+    sources = jnp.where(vlist_src >= 0, slot * rows + vlist_src % rows, -1)
+    local_field = interact(window, sources, vlist_type, transfer, half_width)
     return (upward, local_field)
 
 

time: 115 us -> 83.4 us (0.73)
  the two profiles are of different devices: /device:TPU:0 before, /device:TPU:1 now
where the time goes in v2:
time: 83.4 us; the launch traced here: 82 us
  Pallas kernels  60.7 us (73%)
  matrix products  8.68 us (10%)
  local copies, waits for them, and re-layouts  3.93 us (5%)
  other arithmetic  3.46 us (4%)
  waiting for transfers between devices  2.37 us (3%)
  starting transfers between devices  1.97 us (2%)
  between operations  0.88 us (1%)
    pallas_call x1, Pallas kernels, interact(): pl.pallas_call(functools.partial(interact_kernel, fixed, CHUNK, half_widt...  35.2 us
    pallas_call x1, Pallas kernels, exchange(): pl.pallas_call(functools.partial(exchange_kernel, axis, lax.axis_size(axi...  25.5 us
    ppermute x1, waiting for transfers between devices, passed_along(): lax.ppermute(value, axis, [(source, source + steps) for source in range(f...  2.37 us
    dot_general x1, matrix products, shards(): jnp.dot(imag_b, coarsen[1], preferred_element_type=jnp.float32)  2.24 us
    dot_general x1, matrix products, shards(): jnp.dot(real_b, coarsen[1], preferred_element_type=jnp.float32)  2.05 us
    ppermute x1, starting transfers between devices, passed_along(): lax.ppermute(value, axis, [(source, source + steps) for source in range(f...  1.97 us
    unnamed x15, local copies, waits for them, and re-layouts  1.89 us
  transfers between devices with their start and end apart: 1, of which 1 were waited for; matrix products, arithmetic and copies ran while one was open for 2% of the time, Pallas kernels for 0%

profile of v2, /device:TPU:1, one launch (start us, length us, event | category | flops | bytes accessed | tf_op | source)
XLA Modules:
  0.0 82.0 jit_solution(15438779848820508451)
XLA Ops:
  0.6 0.0 copy-start.5
  0.6 0.0 copy-start.6
  0.7 0.9 %fusion.50 = (f32[8,1008]{1,0:T(8,128)S(1)}, f32[8,1008]{1,0:T(8,128)S(1)}) fusion(f32[8,1008]{1,0:T(8,128)} %param.11), kind=kLoop, calls=%fused_computation.73 | loop fusion | bytes 96768 | tf_op jit(solution)/shard_map/cos | solution.py:234
  1.6 0.7 and_select_fusion.1
  2.2 1.4 %convert_element_type.6 = f32[256,2016]{0,1:T(8,128)S(1)} convert(bf16[256,2016]{0,1:T(8,128)(2,1)} %param.8) | non-fusion elementwise | flops 516096 | bytes 3096576 | tf_op jit(solution)/shard_map/convert_element_type | solution.py:239
  3.6 0.0 copy-done.5
  3.6 0.0 copy-done.6
  3.7 1.2 %fusion.27 = f32[256,2016]{0,1:T(8,128)S(1)} fusion(f32[8,1008]{1,0:T(8,128)S(1)} %get-tuple-element.13, f32[8,1008]{1,0:T(8,128)S(1)} %get-tuple-element.12, s32[256]{0:T(256)S(1)} %and_select_fusion.1), kind=kOutput, calls=%fused_computation.29 | convolution fusion | flops 49563392 | bytes 2129920 | tf_op jit(solution)/shard_map/dot_general | solution.py:236
  4.9 0.3 multiply_subtract_fusion
  5.2 0.0 copy-start.3
  5.2 0.0 copy-start.4
  5.2 1.0 %fusion.12 = f32[1,2016]{1,0:T(1,128)S(1)} fusion(pred[256,1]{0,1:T(4,128)(4,1)S(1)} %reshape.20, f32[256,1008]{0,1:T(8,128)S(1)} %get-tuple-element.9, f32[256,1008]{0,1:T(8,128)S(1)} %get-tuple-element.8), kind=kOutput, calls=%fused_computation.13 | convolution fusion | flops 6709248 | bytes 2072704 | tf_op jit(solution)/shard_map/dot_general | solution.py:248
  6.2 2.0 %collective-permute-start = (f32[2016]{0:T(1024)S(1)}, f32[2016]{0:T(1024)S(1)}, u32[]{:S(2)}, u32[]{:S(2)}) collective-permute-start(f32[2016]{0:T(1024)S(1)} %bitcast.29), channel_id=1, source_target_pairs={{1,0},{2,1},{3,2},{4,3},{5,4},{6,5},{7,6},{8,7},{9,8},{10,9},{11,1... | collective-permute-start | bytes 24200 | tf_op jit(solution)/shard_map/ppermute | solution.py:18
  8.2 1.2 %fusion.13 = f32[64,2016]{1,0:T(8,128)S(1)} fusion(f32[256,1008]{0,1:T(8,128)S(1)} %get-tuple-element.9, f32[256,1008]{0,1:T(8,128)S(1)} %get-tuple-element.8, s32[64]{0:T(128)S(1)} %copy-done.6, s32[256]{0:T(256)S(1)} %get-tuple-element.7), kind=kOutput, calls=%fused_computation.14 | convolution fusion | flops 396910592 | bytes 2581760 | tf_op jit(solution)/shard_map/lp,lc->pc/dot_general | solution.py:246
  9.4 0.0 copy-done.3
  9.4 0.0 copy-done.4
  9.4 0.1 broadcast_select_fusion
  9.5 0.1 broadcast_select_fusion.1
  9.7 2.4 %collective-permute-done = f32[2016]{0:T(1024)S(1)} collective-permute-done((f32[2016]{0:T(1024)S(1)}, f32[2016]{0:T(1024)S(1)}, u32[]{:S(2)}, u32[]{:S(2)}) %collective-permute-start) | collective-permute-done | bytes 8096 | tf_op jit(solution)/shard_map/ppermute | solution.py:18
  12.1 0.0 copy-start.2
  12.1 2.2 %fusion.2 = f32[64,1008]{1,0:T(8,128)S(1)} fusion(bf16[2,1008,1008]{2,1,0:T(8,128)(2,1)} %param.12, bf16[1,2016]{1,0:T(2,128)(2,1)S(1)} %fusion.41, bf16[63,2016]{1,0:T(8,128)(2,1)S(1)} %slice.101), kind=kOutput, calls=%fused_computation.3 | convolution fusion | flops 130314240 | bytes 2580480 | tf_op jit(solution)/shard_map/dot_general | solution.py:254
  14.4 2.1 %fusion = f32[64,1008]{1,0:T(8,128)S(1)} fusion(bf16[2,1008,1008]{2,1,0:T(8,128)(2,1)} %param.12, bf16[63,2016]{1,0:T(8,128)(2,1)S(1)} %slice.101, bf16[1,2016]{1,0:T(2,128)(2,1)S(1)} %fusion.41), kind=kOutput, calls=%fused_computation.1 | convolution fusion | flops 130314240 | bytes 2580480 | tf_op jit(solution)/shard_map/dot_general | solution.py:257
  16.4 0.0 copy-done.2
  16.4 0.5 fusion.23
  16.9 0.5 fusion.20
  17.5 0.0 copy-start.1
  17.5 0.8 pad_maximum_fusion.3
  18.3 0.3 copy.11
  18.6 0.2 pad.13.clone
  18.8 0.9 %reshape.18.own_ref = bf16[64,16,128]{2,1,0:T(8,128)(2,1)} reshape(bf16[64,2,1024]{2,1,0:T(2,128)(2,1)S(1)} %pad.13.clone) | data formatting | bytes 524288 | tf_op jit(solution)/shard_map/reshape | solution.py:25
  19.7 25.5 %exchange.1 = (bf16[8,64,16,128]{3,2,1,0:T(8,128)(2,1)}, bf16[64,16,128]{2,1,0:T(8,128)(2,1)}) custom-call(bf16[64,16,128]{2,1,0:T(8,128)(2,1)} %reshape.18.own_ref), custom_call_target="tpu_custom_call" | custom-call | tf_op jit(solution)/shard_map/exchange/pallas_call | solution.py:119
  45.2 0.0 copy-done.1
  45.2 0.0 copy-start
  45.2 1.6 %copy-done = bf16[8,64,16,128]{3,2,1,0:T(8,128)(2,1)S(1)} copy-done((bf16[8,64,16,128]{3,2,1,0:T(8,128)(2,1)S(1)}, bf16[8,64,16,128]{3,2,1,0:T(8,128)(2,1)}, u32[]{:S(2)}) %copy-start) | copy-done | bytes 2097176
  46.8 35.2 %interact.1 = bf16[64,2016]{1,0:T(8,128)(2,1)} custom-call(s32[64]{0:T(128)S(1)} %and_select_fusion.count_ref, s32[64,192]{1,0:T(8,128)S(1)} %pad.11.src_ref, s32[64,192]{1,0:T(8,128)S(1)} %pad.12.kind_ref, bf16[512,16,128]{2,1,0:T(8,128)(2,1)S(1)} %bitcast.26, bf16[316,2016]{1,0:T(8,128)(2,1)S(1)} %copy-done.1), custom_call_target="tpu_custom_call" | custom-call | tf_op jit(solution)/shard_map/interact/pallas_call | solution.py:213
  (8 shorter events, 0.2 us)
Async XLA Ops:
  0.6 3.0 %copy-start.5 = (s32[256]{0:T(256)S(1)}, s32[256]{0:T(256)}, u32[]{:S(2)}) copy-start(s32[256]{0:T(256)} %param.9) | copy-start | bytes 3076
  0.6 3.0 %copy-start.6 = (s32[64]{0:T(128)S(1)}, s32[64]{0:T(128)}, u32[]{:S(2)}) copy-start(s32[64]{0:T(128)} %param.10) | copy-start | bytes 772
  5.2 4.2 %copy-start.3 = (s32[64,189]{1,0:T(8,128)S(1)}, s32[64,189]{1,0:T(8,128)}, u32[]{:S(2)}) copy-start(s32[64,189]{1,0:T(8,128)} %param.15) | copy-start | bytes 145156
  5.2 4.2 %copy-start.4 = (s32[64,189]{1,0:T(8,128)S(1)}, s32[64,189]{1,0:T(8,128)}, u32[]{:S(2)}) copy-start(s32[64,189]{1,0:T(8,128)} %param.14) | copy-start | bytes 145156
  6.2 5.8 %collective-permute-start = (f32[2016]{0:T(1024)S(1)}, f32[2016]{0:T(1024)S(1)}, u32[]{:S(2)}, u32[]{:S(2)}) collective-permute-start(f32[2016]{0:T(1024)S(1)} %bitcast.29), channel_id=1, source_target_pairs={{1,0},{2,1},{3,2},{4,3},{5,4},{6,5},{7,6},{8,7},{9,8},{10,9},{11,1... | collective-permute-start | bytes 24200 | tf_op jit(solution)/shard_map/ppermute | solution.py:18
  12.1 4.3 %copy-start.2 = (bf16[2,1008,1008]{2,1,0:T(8,128)(2,1)S(1)}, bf16[2,1008,1008]{2,1,0:T(8,128)(2,1)}, u32[]{:S(2)}) copy-start(bf16[2,1008,1008]{2,1,0:T(8,128)(2,1)} %param.12) | copy-start | bytes 12192772
  17.5 27.7 %copy-start.1 = (bf16[316,2016]{1,0:T(8,128)(2,1)S(1)}, bf16[316,2016]{1,0:T(8,128)(2,1)}, u32[]{:S(2)}) copy-start(bf16[316,2016]{1,0:T(8,128)(2,1)} %transfer_ref.1) | copy-start | bytes 3822340
  45.2 1.6 %copy-start = (bf16[8,64,16,128]{3,2,1,0:T(8,128)(2,1)S(1)}, bf16[8,64,16,128]{3,2,1,0:T(8,128)(2,1)}, u32[]{:S(2)}) copy-start(bf16[8,64,16,128]{3,2,1,0:T(8,128)(2,1)} %get-tuple-element.3) | copy-start | bytes 6291460

commit v3 on v2

v3 whole, which is shorter than its diff:
```python
import functools
import jax
import jax.numpy as jnp
from jax import lax
from jax.experimental import pallas as pl
from jax.experimental.pallas import tpu as pltpu
from jax.sharding import PartitionSpec as P

GBITS = 3
LANES = 128
CHUNK = 16
PARTS = 4


def upward_kernel(
    axis, count, group, keys_ref, wanted_ref, phase_ref, leaf_ref, coarsen_ref, up_ref, window_ref, prev_ref,
    coarsen_here, tail_out, tail_in, own_wide, own_ref, *sems
):
    (z_send, z_recv, far_send, far_recv, near_send, near_recv, pass_send, pass_recv,
     own_sem, coarsen_sem, tail_send, tail_recv) = sems
    coarsen_copy = pltpu.make_async_copy(coarsen_ref, coarsen_here, coarsen_sem)
    coarsen_copy.start()
    me = lax.axis_index(axis)
    r = lax.rem(me, group)
    base = me - r
    after = lax.rem(me + group, count)
    before = lax.rem(me + count - group, count)
    twin = me + 1 - 2 * lax.rem(r, 2)
    steps = range(2, group, 2)
    piece = own_ref.shape[0] // PARTS

    barrier = pltpu.get_barrier_semaphore()
    left, right = lax.rem(me + count - 1, count), lax.rem(me + 1, count)
    greeted = [after, before, twin, left, right] + [base + lax.rem(r + step, group) for step in steps]
    for device in greeted:
        pl.semaphore_signal(barrier, inc=1, device_id={axis: device}, device_id_type=pl.DeviceIdType.MESH)
    pl.semaphore_wait(barrier, len(greeted))

    def copy(source, target, send, recv, device):
        return pltpu.make_async_remote_copy(
            src_ref=source, dst_ref=target, send_sem=send, recv_sem=recv,
            device_id={axis: device}, device_id_type=pl.DeviceIdType.MESH,
        )

    def rows_of(part):
        return pl.ds(part * piece, piece)

    def along(part):
        return copy(own_ref.at[rows_of(part)], prev_ref.at[rows_of(part)], z_send.at[part], z_recv.at[part], after)

    def far(block, index, part):
        peer = base + lax.rem(r + steps[index], group)
        return copy(
            block.at[rows_of(part)], window_ref.at[r, rows_of(part)],
            far_send.at[index, part], far_recv.at[index, part], peer,
        )

    def near(block, part):
        return copy(
            block.at[rows_of(part)], window_ref.at[r, rows_of(part)], near_send.at[part], near_recv.at[part], twin
        )

    def onward(index, part):
        slot = lax.rem(r + group - steps[index], group)
        here = window_ref.at[slot, rows_of(part)]
        return copy(here, here, pass_send.at[index, part], pass_recv.at[index, part], twin)

    half_width = phase_ref.shape[1]
    codes = phase_ref.shape[0]
    rows = own_ref.shape[0]
    cosine, sine = jnp.cos(phase_ref[...]), jnp.sin(phase_ref[...])
    keys = keys_ref[...]
    real_in, imag_in = leaf_ref[:, :half_width], leaf_ref[:, half_width:]

    def selected(mask):
        picker = jnp.where(mask, 1.0, 0.0).astype(jnp.bfloat16)
        real = jnp.dot(picker, real_in, preferred_element_type=jnp.float32)
        return real, jnp.dot(picker, imag_in, preferred_element_type=jnp.float32)

    code = lax.broadcasted_iota(jnp.int32, (codes, keys.shape[1]), 0)
    real, imag = selected(((keys & (codes - 1)) == code) & (keys < wanted_ref[0:1, :]))
    tail_out[0:1, :half_width] = jnp.sum(real * cosine - imag * sine, 0, keepdims=True)
    tail_out[1:2, :half_width] = jnp.sum(real * sine + imag * cosine, 0, keepdims=True)
    tail_copy = copy(tail_out, tail_in, tail_send, tail_recv, left)
    tail_copy.start()

    real, imag = selected(wanted_ref[...] == keys)
    real_sum = jnp.zeros((rows, half_width), jnp.float32)
    imag_sum = jnp.zeros((rows, half_width), jnp.float32)
    for c in range(codes):
        a, b = real[c * rows : (c + 1) * rows], imag[c * rows : (c + 1) * rows]
        real_sum = real_sum + (a * cosine[c : c + 1] - b * sine[c : c + 1])
        imag_sum = imag_sum + (a * sine[c : c + 1] + b * cosine[c : c + 1])
    tail_copy.wait_recv()
    last = lax.broadcasted_iota(jnp.int32, (rows, 1), 0) == rows - 1
    real_sum = real_sum + jnp.where(last, tail_in[0:1, :half_width], 0.0)
    imag_sum = imag_sum + jnp.where(last, tail_in[1:2, :half_width], 0.0)
    gathered = jnp.concatenate([real_sum, imag_sum], 0).astype(jnp.bfloat16)
    coarsen_copy.wait()
    by_real = jnp.dot(gathered, coarsen_here[0], preferred_element_type=jnp.float32)
    by_imag = jnp.dot(gathered, coarsen_here[1], preferred_element_type=jnp.float32)
    outs = (by_real[:rows] - by_imag[rows:], by_imag[:rows] + by_real[rows:])
    tiles = own_wide.shape[1] // 2
    padding = jnp.zeros((rows, tiles * LANES - half_width), jnp.float32)
    for part in range(2):
        whole = jnp.concatenate([outs[part], padding], 1)
        for i in range(tiles):
            own_wide[:, part * tiles + i, :] = whole[:, i * LANES : (i + 1) * LANES]
    own_ref[...] = own_wide[...].astype(own_ref.dtype)

    parts = range(PARTS)
    indices = range(len(steps))
    @pl.when(r > 0)
    def _():
        for part in parts:
            along(part).start()
    for part in parts:
        for index in indices:
            @pl.when(r + steps[index] < group)
            def _():
                far(own_ref, index, part).start()
    @pl.when(lax.rem(r, 2) == 0)
    def _():
        for part in parts:
            near(own_ref, part).start()
    own_copy = pltpu.make_async_copy(own_ref, window_ref.at[r], own_sem)
    own_copy.start()
    for part in range(2):
        up_ref[:, part * half_width : (part + 1) * half_width] = outs[part].astype(up_ref.dtype)
    for part in parts:
        @pl.when(r > 0)
        def _():
            along(part).wait_recv()
        for index in indices:
            @pl.when(r + steps[index] >= group)
            def _():
                far(prev_ref, index, part).start()
        @pl.when(lax.rem(r, 2) == 1)
        def _():
            near(prev_ref, part).start()
    for index in indices:
        for part in parts:
            far(own_ref, index, part).wait_recv()
            onward(index, part).start()
    for part in parts:
        near(own_ref, part).wait_recv()
        for index in indices:
            onward(index, part).wait_recv()
    tail_copy.wait_send()
    for part in parts:
        @pl.when(r > 0)
        def _():
            along(part).wait_send()
        near(own_ref, part).wait_send()
        for index in indices:
            far(own_ref, index, part).wait_send()
            onward(index, part).wait_send()
    own_copy.wait()


def upward_and_window(leaf_spectra, leaf_keys, parent_keys, child_phase, coarsen, axis, group):
    half_width = child_phase.shape[1]
    rows = parent_keys.shape[0]
    codes = child_phase.shape[0]
    tiles = 2 * (-(-half_width // LANES))
    wanted = (jnp.arange(codes, dtype=jnp.int32)[:, None] + codes * parent_keys[None, :]).reshape(-1, 1)
    others = group // 2 - 1
    dma = pltpu.SemaphoreType.DMA
    anywhere = pl.BlockSpec(memory_space=pl.ANY)
    vmem = pl.BlockSpec(memory_space=pltpu.VMEM)
    own = (rows, tiles, LANES)
    upward, window, _ = pl.pallas_call(
        functools.partial(upward_kernel, axis, lax.axis_size(axis), group),
        out_shape=[
            jax.ShapeDtypeStruct((rows, 2 * half_width), jnp.bfloat16),
            jax.ShapeDtypeStruct((group,) + own, jnp.bfloat16),
            jax.ShapeDtypeStruct(own, jnp.bfloat16),
        ],
        in_specs=[vmem, vmem, vmem, vmem, anywhere],
        out_specs=[vmem, anywhere, anywhere],
        scratch_shapes=[
            pltpu.VMEM(coarsen.shape, coarsen.dtype),
            pltpu.VMEM((2, tiles // 2 * LANES), jnp.float32),
            pltpu.VMEM((2, tiles // 2 * LANES), jnp.float32),
            pltpu.VMEM(own, jnp.float32),
            pltpu.VMEM(own, jnp.bfloat16),
            dma((PARTS,)), dma((PARTS,)),
            dma((others, PARTS)), dma((others, PARTS)),
            dma((PARTS,)), dma((PARTS,)),
            dma((others, PARTS)), dma((others, PARTS)),
            dma, dma, dma, dma,
        ],
        compiler_params=pltpu.CompilerParams(
            collective_id=0, has_side_effects=True, vmem_limit_bytes=32 * 2**20
        ),
        name="upward_and_window",
    )(leaf_keys.reshape(1, -1), wanted, child_phase, leaf_spectra, coarsen)
    return upward, window


def interact_kernel(
    fixed, chunk, half_width, count_ref, src_ref, kind_ref, window_ref, transfer_ref, out_ref, table, coef, sums,
    window_here, window_sem
):
    rows = table.shape[1]
    half = rows // 2
    kinds = transfer_ref.shape[0]
    step = 16

    window_copy = pltpu.make_async_copy(window_ref, window_here, window_sem)
    window_copy.start()

    def widen(i, carry):
        part = pl.ds(pl.multiple_of(i * step, step), step)
        table[part] = window_here[part].astype(jnp.float32)
        return carry

    def lay_out(start, count):
        block = transfer_ref[pl.ds(start, count), :].astype(jnp.float32)
        for part in range(2):
            whole = block[:, part * half_width : (part + 1) * half_width]
            whole = jnp.concatenate([whole, jnp.zeros((count, half * LANES - half_width), jnp.float32)], 1)
            for i in range(half):
                coef[pl.ds(start, count), part * half + i, :] = whole[:, i * LANES : (i + 1) * LANES]

    def lay_out_step(i, carry):
        lay_out(pl.multiple_of(i * step, step), step)
        return carry

    even = kinds // step
    lax.fori_loop(0, even, lay_out_step, 0)
    if kinds % step:
        lay_out(even * step, kinds % step)
    coef[kinds] = jnp.zeros(coef.shape[1:], jnp.float32)
    window_copy.wait()
    lax.fori_loop(0, table.shape[0] // step, widen, 0)

    def some_slots(target, first, count, acc):
        re, im = acc
        for slot in range(count):
            source = table[src_ref[target, first + slot]]
            factor = coef[kind_ref[target, first + slot]]
            re = re + (factor[:half] * source[:half] - factor[half:] * source[half:])
            im = im + (factor[:half] * source[half:] + factor[half:] * source[:half])
        return re, im

    most = (src_ref.shape[1] - fixed) // chunk

    def one_target(target, carry):
        def exactly(chunks):
            zero = jnp.zeros((half, LANES), jnp.float32)
            acc = some_slots(target, 0, fixed + chunks * chunk, (zero, zero))
            sums[target, :half] = acc[0]
            sums[target, half:] = acc[1]

        def between(low, high):
            if low == high:
                exactly(low)
                return
            middle = (low + high) // 2
            lax.cond(more <= middle, lambda: between(low, middle), lambda: between(middle + 1, high))

        more = count_ref[target]
        between(0, most)
        return carry

    lax.fori_loop(0, src_ref.shape[0], one_target, 0)
    for part in range(2):
        pieces = [sums[:, part * half + i, :] for i in range(half)]
        whole = jnp.concatenate(pieces, 1)[:, :half_width]
        out_ref[:, part * half_width : (part + 1) * half_width] = whole.astype(out_ref.dtype)


def interact(window, sources, kinds, transfer, half_width):
    rows = window.shape[1]
    targets, slots = sources.shape
    kinds_count = transfer.shape[0]
    fixed = -(-(slots // 2) // CHUNK) * CHUNK
    padded = fixed + -(-(slots - fixed) // CHUNK) * CHUNK
    live = sources >= 0
    tail = ((0, 0), (0, padded - slots))
    src = jnp.pad(jnp.where(live, sources, 0), tail)
    kind = jnp.pad(jnp.where(live, kinds, kinds_count), tail, constant_values=kinds_count)
    lengths = jnp.sum(live.astype(jnp.int32), 1)
    more = jnp.maximum(lengths - fixed + CHUNK - 1, 0) // CHUNK
    smem = pl.BlockSpec(memory_space=pltpu.SMEM)
    vmem = pl.BlockSpec(memory_space=pltpu.VMEM)
    return pl.pallas_call(
        functools.partial(interact_kernel, fixed, CHUNK, half_width),
        out_shape=jax.ShapeDtypeStruct((targets, 2 * half_width), jnp.bfloat16),
        in_specs=[smem, smem, smem, pl.BlockSpec(memory_space=pl.ANY), vmem],
        out_specs=vmem,
        scratch_shapes=[
            pltpu.VMEM(window.shape, jnp.float32),
            pltpu.VMEM((kinds_count + 1, rows, LANES), jnp.float32),
            pltpu.VMEM((targets, rows, LANES), jnp.float32),
            pltpu.VMEM(window.shape, window.dtype),
            pltpu.SemaphoreType.DMA,
        ],
        compiler_params=pltpu.CompilerParams(vmem_limit_bytes=32 * 2**20),
        name="interact",
    )(more, src, kind, window, transfer)


def shards(
    leaf_spectra, leaf_keys, parent_keys, child_phase, coarsen, transfer, vlist_src, vlist_type
):
    half_width = child_phase.shape[1]
    group = 2**GBITS
    upward, window = upward_and_window(
        leaf_spectra, leaf_keys, parent_keys, child_phase, coarsen, "oct", group
    )
    rows = parent_keys.shape[0]
    window = window.reshape((group * rows,) + window.shape[2:])
    rank = lax.rem(lax.axis_index("oct"), group)
    slot = (vlist_src // rows + rank + 1) % group
    sources = jnp.where(vlist_src >= 0, slot * rows + vlist_src % rows, -1)
    local_field = interact(window, sources, vlist_type, transfer, half_width)
    return (upward, local_field)


def solution(mesh):
    return jax.shard_map(
        shards,
        mesh=mesh,
        in_specs=(
            P("oct", None),
            P("oct"),
            P("oct"),
            P(),
            P(),
            P(),
            P("oct", None),
            P("oct", None),
        ),
        out_specs=(P("oct", None), P("oct", None)),
        check_vma=False,
    )
```

time: 83.4 us -> 67.9 us (0.81)
  matrix products: 8.68 us -> 0 us
  local copies, waits for them, and re-layouts: 3.93 us -> 6.6 us
  Pallas kernels: 60.7 us -> 58.2 us
  waiting for transfers between devices: 2.37 us -> 0 us
  starting transfers between devices: 1.97 us -> 0 us
  other arithmetic: 3.46 us -> 1.74 us
    dot_general x7 -> x0, matrix products: 8.68 us -> none  [the longest x1 2.24 us: shards(): jnp.dot(imag_b, coarsen[1], preferred_element_type=jnp.float32)]
    pallas_call x1, Pallas kernels: 35.2 us -> 29.9 us  [interact(): pl.pallas_call(functools.partial(interact_kernel, fixed, CHUNK, half_widt...]
    unnamed x15 -> x16, local copies, waits for them, and re-layouts: 1.89 us -> 6.38 us
    pallas_call x1, Pallas kernels: 25.5 us -> 28.3 us  [upward_and_window(): pl.pallas_call(functools.partial(upward_kernel, axis, lax.axis_size(axis)...]
    ppermute x1 -> x0, waiting for transfers between devices: 2.37 us -> none  [passed_along(): lax.ppermute(value, axis, [(source, source + steps) for source in range(f...]
    ppermute x1 -> x0, starting transfers between devices: 1.97 us -> none  [passed_along(): lax.ppermute(value, axis, [(source, source + steps) for source in range(f...]
    convert_element_type x1 -> x0, other arithmetic: 1.37 us -> none  [shards(): spectra = leaf_spectra.astype(jnp.float32)]
    cos x1 -> x0, local copies, waits for them, and re-layouts: 0.9 us -> none  [shards(): jnp.cos(child_phase)]
  transfers between devices with their start and end apart: 1 -> 0, of which waited for: 1 -> 0; matrix products, arithmetic and copies ran while one was open for 2% -> 0% of each run, Pallas kernels for 0% -> 0%
where the time goes in v3:
time: 67.9 us; the launch traced here: 67.3 us
  Pallas kernels  58.2 us (86%)
  local copies, waits for them, and re-layouts  6.6 us (10%)
  other arithmetic  1.74 us (3%)
  between operations  0.76 us (1%)
    pallas_call x1, Pallas kernels, interact(): pl.pallas_call(functools.partial(interact_kernel, fixed, CHUNK, half_widt...  29.9 us
    pallas_call x1, Pallas kernels, upward_and_window(): pl.pallas_call(functools.partial(upward_kernel, axis, lax.axis_size(axis)...  28.3 us
    unnamed x16, local copies, waits for them, and re-layouts  6.38 us

profile of v3, /device:TPU:1, one launch (start us, length us, event | category | flops | bytes accessed | tf_op | source)
XLA Modules:
  0.0 67.3 jit_solution(11188724522959151613)
XLA Ops:
  0.6 0.0 copy-start.5
  0.6 0.0 copy-start.4
  0.7 0.7 broadcast_multiply_fusion
  1.3 0.2 add.70.wanted_ref
  1.5 1.5 %copy.12.leaf_ref = bf16[256,2016]{1,0:T(8,128)(2,1)S(1)} copy(bf16[256,2016]{0,1:T(8,128)(2,1)} %param.8) | data formatting | bytes 2064384 | tf_op args[0]
  3.0 0.0 copy-done.5
  3.0 0.0 copy-done.4
  3.0 0.0 copy-start
  3.1 2.2 %copy-done = bf16[2,1008,1008]{2,1,0:T(8,128)(2,1)S(1)} copy-done((bf16[2,1008,1008]{2,1,0:T(8,128)(2,1)S(1)}, bf16[2,1008,1008]{2,1,0:T(8,128)(2,1)}, u32[]{:S(2)}) %copy-start) | copy-done | bytes 4064280
  5.2 0.0 copy-start.6
  5.2 28.3 %upward_and_window.1 = (bf16[64,2016]{1,0:T(8,128)(2,1)S(1)}, bf16[8,64,16,128]{3,2,1,0:T(8,128)(2,1)S(1)}, bf16[64,16,128]{2,1,0:T(8,128)(2,1)}) custom-call(s32[1,256]{1,0:T(1,128)S(1)} %bitcast.3, s32[512,1]{1,0:T(8,128)S(1)} %add.70.wanted_ref, f32[8,1008]{1,0:T(8,128)S(1)} %copy-done.4, bf16[256,2016]{1,0:T(8,128)(2,1)S(1)} %copy.12.leaf_ref, ...), custom_call_target="tpu_custom_call" | custom-call | tf_op jit(solution)/shard_map/upward_and_window/pallas_call | solution.py:172
  33.5 0.0 copy-start.2
  33.5 0.7 %copy-done.2 = bf16[64,2016]{1,0:T(8,128)(2,1)} copy-done((bf16[64,2016]{1,0:T(8,128)(2,1)}, bf16[64,2016]{1,0:T(8,128)(2,1)S(1)}, u32[]{:S(2)}) %copy-start.2) | copy-done | bytes 258072
  34.2 0.0 copy-done.6
  34.2 0.9 %broadcast_select_fusion = (s32[64,189]{1,0:T(8,128)S(1)}, s32[64,189]{1,0:T(8,128)S(1)}) fusion(s32[64,189]{1,0:T(8,128)S(1)} %copy-done.6, s32[]{:T(128)S(6)} %rem.75, s32[64,189]{1,0:T(8,128)} %param.14), kind=kLoop, calls=%fused_computation.17 | loop fusion | flops 459648 | bytes 193540 | tf_op jit(solution)/shard_map/jit(_where)/select_n | solution.py:283
  35.2 0.0 copy-start.3
  35.2 0.1 broadcast_select_fusion.1
  35.3 0.0 copy-start.1
  35.4 1.3 %copy-done.1 = bf16[316,2016]{1,0:T(8,128)(2,1)S(1)} copy-done((bf16[316,2016]{1,0:T(8,128)(2,1)S(1)}, bf16[316,2016]{1,0:T(8,128)(2,1)}, u32[]{:S(2)}) %copy-start.1) | copy-done | bytes 1274136
  36.7 29.9 %interact.1 = bf16[64,2016]{1,0:T(8,128)(2,1)} custom-call(s32[64]{0:T(128)S(1)} %and_select_fusion.count_ref, s32[64,192]{1,0:T(8,128)S(1)} %pad.7.src_ref, s32[64,192]{1,0:T(8,128)S(1)} %pad.8.kind_ref, bf16[512,16,128]{2,1,0:T(8,128)(2,1)S(1)} %bitcast.2, bf16[316,2016]{1,0:T(8,128)(2,1)S(1)} %copy-done.1), custom_call_target="tpu_custom_call" | custom-call | tf_op jit(solution)/shard_map/interact/pallas_call | solution.py:288
  66.6 0.0 copy-done.3
  66.6 0.7 %copy.14 = bf16[64,2016]{1,0:T(8,128)(2,1)} copy(bf16[64,2016]{1,0:T(8,128)(2,1)S(1)} %copy-done.3) | data formatting | bytes 516096
  (4 shorter events, 0.0 us)
Async XLA Ops:
  0.6 2.4 %copy-start.5 = (s32[256]{0:T(256)S(1)}, s32[256]{0:T(256)}, u32[]{:S(2)}) copy-start(s32[256]{0:T(256)} %param.9) | copy-start | bytes 3076
  0.6 2.4 %copy-start.4 = (f32[8,1008]{1,0:T(8,128)S(1)}, f32[8,1008]{1,0:T(8,128)}, u32[]{:S(2)}) copy-start(f32[8,1008]{1,0:T(8,128)} %phase_ref.1) | copy-start | bytes 96772
  3.0 2.2 %copy-start = (bf16[2,1008,1008]{2,1,0:T(8,128)(2,1)S(1)}, bf16[2,1008,1008]{2,1,0:T(8,128)(2,1)}, u32[]{:S(2)}) copy-start(bf16[2,1008,1008]{2,1,0:T(8,128)(2,1)} %coarsen_ref.1) | copy-start | bytes 12192772
  5.2 29.0 %copy-start.6 = (s32[64,189]{1,0:T(8,128)S(1)}, s32[64,189]{1,0:T(8,128)}, u32[]{:S(2)}) copy-start(s32[64,189]{1,0:T(8,128)} %param.15) | copy-start | bytes 145156
  33.5 0.7 %copy-start.2 = (bf16[64,2016]{1,0:T(8,128)(2,1)}, bf16[64,2016]{1,0:T(8,128)(2,1)S(1)}, u32[]{:S(2)}) copy-start(bf16[64,2016]{1,0:T(8,128)(2,1)S(1)} %get-tuple-element.12) | copy-start | bytes 774148
  35.2 31.4 %copy-start.3 = (bf16[64,2016]{1,0:T(8,128)(2,1)S(1)}, bf16[64,2016]{1,0:T(8,128)(2,1)}, u32[]{:S(2)}) copy-start(bf16[64,2016]{1,0:T(8,128)(2,1)} %copy-done.2) | copy-start | bytes 774148
  35.3 1.3 %copy-start.1 = (bf16[316,2016]{1,0:T(8,128)(2,1)S(1)}, bf16[316,2016]{1,0:T(8,128)(2,1)}, u32[]{:S(2)}) copy-start(bf16[316,2016]{1,0:T(8,128)(2,1)} %transfer_ref.1) | copy-start | bytes 3822340

commit v4 on v3

--- a/solution.py
+++ b/solution.py
@@ -13,13 +13,18 @@
 
 
 def upward_kernel(
-    axis, count, group, keys_ref, wanted_ref, phase_ref, leaf_ref, coarsen_ref, up_ref, window_ref, prev_ref,
-    coarsen_here, tail_out, tail_in, own_wide, own_ref, *sems
+    axis, count, group, fixed, chunk, keys_ref, wanted_ref, phase_ref, vsrc_ref, vtype_ref, leaf_hbm, coarsen_hbm,
+    transfer_hbm, up_ref, window_ref, prev_ref, coef_hbm, src_ref, kind_ref, more_ref,
+    leaf_ref, coarsen_ref, transfer_ref, tail_out, tail_in, own_wide, own_ref, coef_wide, coef, *sems
 ):
     (z_send, z_recv, far_send, far_recv, near_send, near_recv, pass_send, pass_recv,
-     own_sem, coarsen_sem, tail_send, tail_recv) = sems
-    coarsen_copy = pltpu.make_async_copy(coarsen_ref, coarsen_here, coarsen_sem)
+     own_sem, leaf_sem, coarsen_sem, transfer_sem, coef_sem, tail_send, tail_recv) = sems
+    leaf_copy = pltpu.make_async_copy(leaf_hbm, leaf_ref, leaf_sem)
+    leaf_copy.start()
+    coarsen_copy = pltpu.make_async_copy(coarsen_hbm, coarsen_ref, coarsen_sem)
     coarsen_copy.start()
+    transfer_copy = pltpu.make_async_copy(transfer_hbm, transfer_ref, transfer_sem)
+    transfer_copy.start()
     me = lax.axis_index(axis)
     r = lax.rem(me, group)
     base = me - r
@@ -70,6 +75,7 @@
     rows = own_ref.shape[0]
     cosine, sine = jnp.cos(phase_ref[...]), jnp.sin(phase_ref[...])
     keys = keys_ref[...]
+    leaf_copy.wait()
     real_in, imag_in = leaf_ref[:, :half_width], leaf_ref[:, half_width:]
 
     def selected(mask):
@@ -97,8 +103,8 @@
     imag_sum = imag_sum + jnp.where(last, tail_in[1:2, :half_width], 0.0)
     gathered = jnp.concatenate([real_sum, imag_sum], 0).astype(jnp.bfloat16)
     coarsen_copy.wait()
-    by_real = jnp.dot(gathered, coarsen_here[0], preferred_element_type=jnp.float32)
-    by_imag = jnp.dot(gathered, coarsen_here[1], preferred_element_type=jnp.float32)
+    by_real = jnp.dot(gathered, coarsen_ref[0], preferred_element_type=jnp.float32)
+    by_imag = jnp.dot(gathered, coarsen_ref[1], preferred_element_type=jnp.float32)
     outs = (by_real[:rows] - by_imag[rows:], by_imag[:rows] + by_real[rows:])
     tiles = own_wide.shape[1] // 2
     padding = jnp.zeros((rows, tiles * LANES - half_width), jnp.float32)
@@ -127,6 +133,41 @@
     own_copy.start()
     for part in range(2):
         up_ref[:, part * half_width : (part + 1) * half_width] = outs[part].astype(up_ref.dtype)
+
+    transfer_copy.wait()
+    kinds = transfer_ref.shape[0]
+    step = coef_wide.shape[0]
+
+    def lay_out(start, size):
+        block = transfer_ref[pl.ds(start, size), :].astype(jnp.float32)
+        padding = jnp.zeros((size, tiles * LANES - half_width), jnp.float32)
+        for part in range(2):
+            whole = jnp.concatenate([block[:, part * half_width : (part + 1) * half_width], padding], 1)
+            for i in range(tiles):
+                coef_wide[pl.ds(0, size), part * tiles + i, :] = whole[:, i * LANES : (i + 1) * LANES]
+        coef[pl.ds(start, size)] = coef_wide[pl.ds(0, size)].astype(coef.dtype)
+
+    def lay_out_step(i, carry):
+        lay_out(pl.multiple_of(i * step, step), step)
+        return carry
+
+    lax.fori_loop(0, kinds // step, lay_out_step, 0)
+    if kinds % step:
+        lay_out(kinds // step * step, kinds % step)
+    coef[kinds] = jnp.zeros(coef.shape[1:], coef.dtype)
+    coef_copy = pltpu.make_async_copy(coef, coef_hbm, coef_sem)
+    coef_copy.start()
+
+    sources = vsrc_ref[...]
+    slots = sources.shape[1]
+    live = sources >= 0
+    place = lax.rem(lax.div(sources, rows) + r + 1, group)
+    src_ref[...] = jnp.zeros(src_ref.shape, jnp.int32)
+    src_ref[:, :slots] = jnp.where(live, place * rows + lax.rem(sources, rows), 0)
+    kind_ref[...] = jnp.full(kind_ref.shape, kinds, jnp.int32)
+    kind_ref[:, :slots] = jnp.where(live, vtype_ref[...], kinds)
+    lengths = jnp.sum(jnp.where(live, 1.0, 0.0), 1, keepdims=True).astype(jnp.int32)
+    more_ref[...] = lax.div(jnp.maximum(lengths - fixed + chunk - 1, 0), chunk)
     for part in parts:
         @pl.when(r > 0)
         def _():
@@ -146,6 +187,7 @@
         near(own_ref, part).wait_recv()
         for index in indices:
             onward(index, part).wait_recv()
+    coef_copy.wait()
     tail_copy.wait_send()
     for part in parts:
         @pl.when(r > 0)
@@ -158,109 +200,87 @@
     own_copy.wait()
 
 
-def upward_and_window(leaf_spectra, leaf_keys, parent_keys, child_phase, coarsen, axis, group):
+def upward_and_window(
+    leaf_spectra, leaf_keys, parent_keys, child_phase, coarsen, transfer, vlist_src, vlist_type, axis, group
+):
     half_width = child_phase.shape[1]
     rows = parent_keys.shape[0]
     codes = child_phase.shape[0]
     tiles = 2 * (-(-half_width // LANES))
     wanted = (jnp.arange(codes, dtype=jnp.int32)[:, None] + codes * parent_keys[None, :]).reshape(-1, 1)
+    slots = vlist_src.shape[1]
+    fixed = slots // 2 // CHUNK * CHUNK
+    padded = -(-slots // CHUNK) * CHUNK
     others = group // 2 - 1
     dma = pltpu.SemaphoreType.DMA
     anywhere = pl.BlockSpec(memory_space=pl.ANY)
     vmem = pl.BlockSpec(memory_space=pltpu.VMEM)
     own = (rows, tiles, LANES)
-    upward, window, _ = pl.pallas_call(
-        functools.partial(upward_kernel, axis, lax.axis_size(axis), group),
+    coef = (transfer.shape[0] + 1, tiles, LANES)
+    upward, window, _, coef, src, kind, more = pl.pallas_call(
+        functools.partial(upward_kernel, axis, lax.axis_size(axis), group, fixed, CHUNK),
         out_shape=[
             jax.ShapeDtypeStruct((rows, 2 * half_width), jnp.bfloat16),
             jax.ShapeDtypeStruct((group,) + own, jnp.bfloat16),
             jax.ShapeDtypeStruct(own, jnp.bfloat16),
+            jax.ShapeDtypeStruct(coef, jnp.bfloat16),
+            jax.ShapeDtypeStruct((rows, padded), jnp.int32),
+            jax.ShapeDtypeStruct((rows, padded), jnp.int32),
+            jax.ShapeDtypeStruct((rows, 1), jnp.int32),
         ],
-        in_specs=[vmem, vmem, vmem, vmem, anywhere],
-        out_specs=[vmem, anywhere, anywhere],
+        in_specs=[vmem] * 5 + [anywhere] * 3,
+        out_specs=[vmem, anywhere, anywhere, anywhere, vmem, vmem, vmem],
         scratch_shapes=[
+            pltpu.VMEM(leaf_spectra.shape, leaf_spectra.dtype),
             pltpu.VMEM(coarsen.shape, coarsen.dtype),
+            pltpu.VMEM(transfer.shape, transfer.dtype),
             pltpu.VMEM((2, tiles // 2 * LANES), jnp.float32),
             pltpu.VMEM((2, tiles // 2 * LANES), jnp.float32),
             pltpu.VMEM(own, jnp.float32),
             pltpu.VMEM(own, jnp.bfloat16),
+            pltpu.VMEM((16, tiles, LANES), jnp.float32),
+            pltpu.VMEM(coef, jnp.bfloat16),
             dma((PARTS,)), dma((PARTS,)),
             dma((others, PARTS)), dma((others, PARTS)),
             dma((PARTS,)), dma((PARTS,)),
             dma((others, PARTS)), dma((others, PARTS)),
-            dma, dma, dma, dma,
+            dma, dma, dma, dma, dma, dma, dma,
         ],
         compiler_params=pltpu.CompilerParams(
-            collective_id=0, has_side_effects=True, vmem_limit_bytes=32 * 2**20
+            collective_id=0, has_side_effects=True, vmem_limit_bytes=56 * 2**20
         ),
         name="upward_and_window",
-    )(leaf_keys.reshape(1, -1), wanted, child_phase, leaf_spectra, coarsen)
-    return upward, window
-
-
-def interact_kernel(
-    fixed, chunk, half_width, count_ref, src_ref, kind_ref, window_ref, transfer_ref, out_ref, table, coef, sums,
-    window_here, window_sem
-):
+    )(
+        leaf_keys.reshape(1, -1), wanted, child_phase, vlist_src, vlist_type, leaf_spectra, coarsen, transfer
+    )
+    return upward, window, coef, src, kind, more, fixed
+
+
+def interact_kernel(fixed, chunk, half_width, count_ref, src_ref, kind_ref, table, coef, out_ref, sums):
     rows = table.shape[1]
     half = rows // 2
-    kinds = transfer_ref.shape[0]
-    step = 16
-
-    window_copy = pltpu.make_async_copy(window_ref, window_here, window_sem)
-    window_copy.start()
-
-    def widen(i, carry):
-        part = pl.ds(pl.multiple_of(i * step, step), step)
-        table[part] = window_here[part].astype(jnp.float32)
-        return carry
-
-    def lay_out(start, count):
-        block = transfer_ref[pl.ds(start, count), :].astype(jnp.float32)
-        for part in range(2):
-            whole = block[:, part * half_width : (part + 1) * half_width]
-            whole = jnp.concatenate([whole, jnp.zeros((count, half * LANES - half_width), jnp.float32)], 1)
-            for i in range(half):
-                coef[pl.ds(start, count), part * half + i, :] = whole[:, i * LANES : (i + 1) * LANES]
-
-    def lay_out_step(i, carry):
-        lay_out(pl.multiple_of(i * step, step), step)
-        return carry
-
-    even = kinds // step
-    lax.fori_loop(0, even, lay_out_step, 0)
-    if kinds % step:
-        lay_out(even * step, kinds % step)
-    coef[kinds] = jnp.zeros(coef.shape[1:], jnp.float32)
-    window_copy.wait()
-    lax.fori_loop(0, table.shape[0] // step, widen, 0)
-
-    def some_slots(target, first, count, acc):
-        re, im = acc
+    most = (src_ref.shape[1] - fixed) // chunk
+
+    def some_slots(target, count):
+        re = jnp.zeros((half, LANES), jnp.float32)
+        im = jnp.zeros((half, LANES), jnp.float32)
         for slot in range(count):
-            source = table[src_ref[target, first + slot]]
-            factor = coef[kind_ref[target, first + slot]]
+            source = table[src_ref[target, slot]].astype(jnp.float32)
+            factor = coef[kind_ref[target, slot]].astype(jnp.float32)
             re = re + (factor[:half] * source[:half] - factor[half:] * source[half:])
             im = im + (factor[:half] * source[half:] + factor[half:] * source[:half])
-        return re, im
-
-    most = (src_ref.shape[1] - fixed) // chunk
+        sums[target, :half] = re
+        sums[target, half:] = im
 
     def one_target(target, carry):
-        def exactly(chunks):
-            zero = jnp.zeros((half, LANES), jnp.float32)
-            acc = some_slots(target, 0, fixed + chunks * chunk, (zero, zero))
-            sums[target, :half] = acc[0]
-            sums[target, half:] = acc[1]
-
         def between(low, high):
             if low == high:
-                exactly(low)
+                some_slots(target, fixed + low * chunk)
                 return
             middle = (low + high) // 2
             lax.cond(more <= middle, lambda: between(low, middle), lambda: between(middle + 1, high))
 
-        more = count_ref[target]
+        more = count_ref[target, 0]
         between(0, most)
         return carry
 
@@ -271,35 +291,19 @@
         out_ref[:, part * half_width : (part + 1) * half_width] = whole.astype(out_ref.dtype)
 
 
-def interact(window, sources, kinds, transfer, half_width):
-    rows = window.shape[1]
-    targets, slots = sources.shape
-    kinds_count = transfer.shape[0]
-    fixed = -(-(slots // 2) // CHUNK) * CHUNK
-    padded = fixed + -(-(slots - fixed) // CHUNK) * CHUNK
-    live = sources >= 0
-    tail = ((0, 0), (0, padded - slots))
-    src = jnp.pad(jnp.where(live, sources, 0), tail)
-    kind = jnp.pad(jnp.where(live, kinds, kinds_count), tail, constant_values=kinds_count)
-    lengths = jnp.sum(live.astype(jnp.int32), 1)
-    more = jnp.maximum(lengths - fixed + CHUNK - 1, 0) // CHUNK
+def interact(window, coef, src, kind, more, fixed, half_width):
+    targets = src.shape[0]
     smem = pl.BlockSpec(memory_space=pltpu.SMEM)
     vmem = pl.BlockSpec(memory_space=pltpu.VMEM)
     return pl.pallas_call(
         functools.partial(interact_kernel, fixed, CHUNK, half_width),
         out_shape=jax.ShapeDtypeStruct((targets, 2 * half_width), jnp.bfloat16),
-        in_specs=[smem, smem, smem, pl.BlockSpec(memory_space=pl.ANY), vmem],
+        in_specs=[smem, smem, smem, vmem, vmem],
         out_specs=vmem,
-        scratch_shapes=[
-            pltpu.VMEM(window.shape, jnp.float32),
-            pltpu.VMEM((kinds_count + 1, rows, LANES), jnp.float32),
-            pltpu.VMEM((targets, rows, LANES), jnp.float32),
-            pltpu.VMEM(window.shape, window.dtype),
-            pltpu.SemaphoreType.DMA,
-        ],
-        compiler_params=pltpu.CompilerParams(vmem_limit_bytes=32 * 2**20),
+        scratch_shapes=[pltpu.VMEM((targets, window.shape[1], LANES), jnp.float32)],
+        compiler_params=pltpu.CompilerParams(vmem_limit_bytes=56 * 2**20),
         name="interact",
-    )(more, src, kind, window, transfer)
+    )(more, src, kind, window, coef)
 
 
 def shards(
@@ -307,15 +311,12 @@
 ):
     half_width = child_phase.shape[1]
     group = 2**GBITS
-    upward, window = upward_and_window(
-        leaf_spectra, leaf_keys, parent_keys, child_phase, coarsen, "oct", group
+    upward, window, coef, src, kind, more, fixed = upward_and_window(
+        leaf_spectra, leaf_keys, parent_keys, child_phase, coarsen, transfer, vlist_src, vlist_type, "oct", group
     )
     rows = parent_keys.shape[0]
     window = window.reshape((group * rows,) + window.shape[2:])
-    rank = lax.rem(lax.axis_index("oct"), group)
-    slot = (vlist_src // rows + rank + 1) % group
-    sources = jnp.where(vlist_src >= 0, slot * rows + vlist_src % rows, -1)
-    local_field = interact(window, sources, vlist_type, transfer, half_width)
+    local_field = interact(window, coef, src, kind, more, fixed, half_width)
     return (upward, local_field)
 
 

time: 67.9 us -> 63 us (0.928)
  local copies, waits for them, and re-layouts: 6.6 us -> 3.88 us
  other arithmetic: 1.74 us -> 0.67 us
    unnamed x16 -> x4, local copies, waits for them, and re-layouts: 6.38 us -> 2.98 us
    pallas_call x1, Pallas kernels: 29.9 us -> 27.8 us  [interact(): pl.pallas_call(functools.partial(interact_kernel, fixed, CHUNK, half_widt...]
    pallas_call x1, Pallas kernels: 28.3 us -> 29.9 us  [upward_and_window(): pl.pallas_call(functools.partial(upward_kernel, axis, lax.axis_size(axis)...]
    select_n x3 -> x0, other arithmetic: 1.06 us -> none  [the longest x1 0.94 us: interact(): jnp.where(live, kinds, kinds_count)]
    add x1, local copies, waits for them, and re-layouts: 0.2 us -> 0.91 us  [upward_and_window(): jnp.arange(codes, dtype=jnp.int32)[:, None] + codes * parent_keys[None, :]]
where the time goes in v4:
time: 63 us; the launch traced here: 62.8 us
  Pallas kernels  57.6 us (91%)
  local copies, waits for them, and re-layouts  3.88 us (6%)
  other arithmetic  0.67 us (1%)
  between operations  0.65 us (1%)
    pallas_call x1, Pallas kernels, upward_and_window(): pl.pallas_call(functools.partial(upward_kernel, axis, lax.axis_size(axis)...  29.9 us
    pallas_call x1, Pallas kernels, interact(): pl.pallas_call(functools.partial(interact_kernel, fixed, CHUNK, half_widt...  27.8 us
    unnamed x4, local copies, waits for them, and re-layouts  2.98 us

profile of v4, /device:TPU:1, one launch (start us, length us, event | category | flops | bytes accessed | tf_op | source)
XLA Modules:
  0.0 62.8 jit_solution(17952661681370964868)
XLA Ops:
  0.6 0.7 %broadcast_multiply_fusion = s32[64]{0:T(128)S(1)} fusion(s32[64]{0:T(128)} %param.10), kind=kLoop, calls=%fused_computation.1 | loop fusion | flops 64 | bytes 512 | tf_op jit(solution)/shard_map/mul | solution.py:210
  1.3 0.9 %add.27.wanted_ref = s32[512,1]{1,0:T(8,128)} reshape(s32[8,64]{1,0:T(8,128)S(1)} %iota_add_fusion) | data formatting | bytes 4096 | tf_op jit(solution)/shard_map/add | solution.py:210
  2.2 2.3 %copy.12.leaf_hbm = bf16[256,2016]{1,0:T(8,128)(2,1)} copy(bf16[256,2016]{0,1:T(8,128)(2,1)} %param.8) | data formatting | bytes 2064384 | tf_op args[0]
  4.5 29.9 %upward_and_window.1 = (bf16[64,2016]{1,0:T(8,128)(2,1)}, bf16[8,64,16,128]{3,2,1,0:T(8,128)(2,1)}, bf16[64,16,128]{2,1,0:T(8,128)(2,1)}, bf16[317,16,128]{2,1,0...) custom-call(s32[1,256]{1,0:T(1,128)} %bitcast.3, s32[512,1]{1,0:T(8,128)} %add.27.wanted_ref, ...), custom_call_target="tpu_custom_call" | custom-call | tf_op jit(solution)/shard_map/upward_and_window/pallas_call | solution.py:220
  34.4 0.0 copy-start
  34.4 27.8 %interact.1 = bf16[64,2016]{1,0:T(8,128)(2,1)} custom-call(s32[64,1]{1,0:T(8,128)} %get-tuple-element.9.count_ref, s32[64,192]{1,0:T(8,128)} %get-tuple-element.10.src_ref, s32[64,192]{1,0:T(8,128)} %get-tuple-element.11.kind_ref, bf16[512,16,128]{2,1,0:T(8,128)(2,1)} %bitcast.2, bf16[317,16,128]{2,1,0:T(8,128)(2,1)} %get-tuple-element.13.coef), custom_call_target="tpu_custom_call" | custom-call | tf_op jit(solution)/shard_map/interact/pallas_call | solution.py:298
  62.1 0.0 copy-done
  62.1 0.7 %copy.14 = bf16[64,2016]{1,0:T(8,128)(2,1)} copy(bf16[64,2016]{1,0:T(8,128)(2,1)S(1)} %copy-done) | data formatting | bytes 516096
  (1 shorter events, 0.0 us)
Async XLA Ops:
  34.4 27.8 %copy-start = (bf16[64,2016]{1,0:T(8,128)(2,1)S(1)}, bf16[64,2016]{1,0:T(8,128)(2,1)}, u32[]{:S(2)}) copy-start(bf16[64,2016]{1,0:T(8,128)(2,1)} %get-tuple-element.16) | copy-start | bytes 774148

commit v5 on v4

--- a/solution.py
+++ b/solution.py
@@ -10,15 +10,16 @@
 LANES = 128
 CHUNK = 16
 PARTS = 4
+CHAINS = 4
 
 
 def upward_kernel(
-    axis, count, group, fixed, chunk, keys_ref, wanted_ref, phase_ref, vsrc_ref, vtype_ref, leaf_hbm, coarsen_hbm,
+    axis, count, group, fixed, chunk, keys_ref, parents_ref, phase_ref, vsrc_ref, vtype_ref, leaf_hbm, coarsen_hbm,
     transfer_hbm, up_ref, window_ref, prev_ref, coef_hbm, src_ref, kind_ref, more_ref,
     leaf_ref, coarsen_ref, transfer_ref, tail_out, tail_in, own_wide, own_ref, coef_wide, coef, *sems
 ):
     (z_send, z_recv, far_send, far_recv, near_send, near_recv, pass_send, pass_recv,
-     own_sem, leaf_sem, coarsen_sem, transfer_sem, coef_sem, tail_send, tail_recv) = sems
+     across_send, across_recv, own_sem, leaf_sem, coarsen_sem, transfer_sem, coef_sem, tail_send, tail_recv) = sems
     leaf_copy = pltpu.make_async_copy(leaf_hbm, leaf_ref, leaf_sem)
     leaf_copy.start()
     coarsen_copy = pltpu.make_async_copy(coarsen_hbm, coarsen_ref, coarsen_sem)
@@ -31,12 +32,22 @@
     after = lax.rem(me + group, count)
     before = lax.rem(me + count - group, count)
     twin = me + 1 - 2 * lax.rem(r, 2)
-    steps = range(2, group, 2)
+    core = lax.rem(r, 2)
+    chip = lax.div(r, 2)
+    flip_low = r + 2 - 4 * lax.rem(chip, 2)
+    flip_high = r + 4 - 8 * lax.div(chip, 2)
+    flip_both = flip_low + flip_high - r
+    peers = (flip_low, flip_high)
+    is_one = jnp.where(chip == 1, 1, 0)
+    is_two = jnp.where(chip == 2, 1, 0)
+    first = 1 - is_one
+    passed = 2 * (2 - 2 * is_one - 2 * is_two - lax.div(chip, 3) + 3 * (is_one * core + is_two * (1 - core))) + core
+    late = is_one * core + is_two * (1 - core)
     piece = own_ref.shape[0] // PARTS
 
     barrier = pltpu.get_barrier_semaphore()
     left, right = lax.rem(me + count - 1, count), lax.rem(me + 1, count)
-    greeted = [after, before, twin, left, right] + [base + lax.rem(r + step, group) for step in steps]
+    greeted = [after, before, twin, left, right] + [base + peer for peer in peers]
     for device in greeted:
         pl.semaphore_signal(barrier, inc=1, device_id={axis: device}, device_id_type=pl.DeviceIdType.MESH)
     pl.semaphore_wait(barrier, len(greeted))
@@ -54,10 +65,9 @@
         return copy(own_ref.at[rows_of(part)], prev_ref.at[rows_of(part)], z_send.at[part], z_recv.at[part], after)
 
     def far(block, index, part):
-        peer = base + lax.rem(r + steps[index], group)
         return copy(
             block.at[rows_of(part)], window_ref.at[r, rows_of(part)],
-            far_send.at[index, part], far_recv.at[index, part], peer,
+            far_send.at[index, part], far_recv.at[index, part], base + peers[index],
         )
 
     def near(block, part):
@@ -65,8 +75,16 @@
             block.at[rows_of(part)], window_ref.at[r, rows_of(part)], near_send.at[part], near_recv.at[part], twin
         )
 
-    def onward(index, part):
-        slot = lax.rem(r + group - steps[index], group)
+    def arrived(index, slot, part):
+        here = window_ref.at[slot, rows_of(part)]
+        return copy(here, here, far_send.at[0, part], far_recv.at[index, part], twin)
+
+    def across(part):
+        here = window_ref.at[passed, rows_of(part)]
+        there = base + 2 * (3 - lax.div(passed, 2)) + core
+        return copy(here, here, across_send.at[part], across_recv.at[part], there)
+
+    def onward(index, slot, part):
         here = window_ref.at[slot, rows_of(part)]
         return copy(here, here, pass_send.at[index, part], pass_recv.at[index, part], twin)
 
@@ -76,21 +94,27 @@
     cosine, sine = jnp.cos(phase_ref[...]), jnp.sin(phase_ref[...])
     keys = keys_ref[...]
     leaf_copy.wait()
-    real_in, imag_in = leaf_ref[:, :half_width], leaf_ref[:, half_width:]
+    real_in, imag_in = leaf_ref[:half_width, :], leaf_ref[half_width:, :]
 
     def selected(mask):
         picker = jnp.where(mask, 1.0, 0.0).astype(jnp.bfloat16)
-        real = jnp.dot(picker, real_in, preferred_element_type=jnp.float32)
-        return real, jnp.dot(picker, imag_in, preferred_element_type=jnp.float32)
+        return tuple(
+            lax.dot_general(picker, half, (((1,), (1,)), ((), ())), preferred_element_type=jnp.float32)
+            for half in (real_in, imag_in)
+        )
 
     code = lax.broadcasted_iota(jnp.int32, (codes, keys.shape[1]), 0)
-    real, imag = selected(((keys & (codes - 1)) == code) & (keys < wanted_ref[0:1, :]))
+    real, imag = selected(((keys & (codes - 1)) == code) & (keys < codes * parents_ref[0:1, 0:1]))
     tail_out[0:1, :half_width] = jnp.sum(real * cosine - imag * sine, 0, keepdims=True)
     tail_out[1:2, :half_width] = jnp.sum(real * sine + imag * cosine, 0, keepdims=True)
     tail_copy = copy(tail_out, tail_in, tail_send, tail_recv, left)
     tail_copy.start()
 
-    real, imag = selected(wanted_ref[...] == keys)
+    square = (rows, rows)
+    diagonal = lax.broadcasted_iota(jnp.int32, square, 0) == lax.broadcasted_iota(jnp.int32, square, 1)
+    parents = jnp.broadcast_to(parents_ref[...].astype(jnp.float32), square)
+    column = codes * jnp.sum(jnp.where(diagonal, parents, 0.0), 1, keepdims=True).astype(jnp.int32)
+    real, imag = selected(jnp.concatenate([column + c for c in range(codes)], 0) == keys)
     real_sum = jnp.zeros((rows, half_width), jnp.float32)
     imag_sum = jnp.zeros((rows, half_width), jnp.float32)
     for c in range(codes):
@@ -115,14 +139,14 @@
     own_ref[...] = own_wide[...].astype(own_ref.dtype)
 
     parts = range(PARTS)
-    indices = range(len(steps))
+    indices = range(len(peers))
     @pl.when(r > 0)
     def _():
         for part in parts:
             along(part).start()
     for part in parts:
         for index in indices:
-            @pl.when(r + steps[index] < group)
+            @pl.when(peers[index] > r)
             def _():
                 far(own_ref, index, part).start()
     @pl.when(lax.rem(r, 2) == 0)
@@ -173,20 +197,28 @@
         def _():
             along(part).wait_recv()
         for index in indices:
-            @pl.when(r + steps[index] >= group)
+            @pl.when(peers[index] < r)
             def _():
                 far(prev_ref, index, part).start()
         @pl.when(lax.rem(r, 2) == 1)
         def _():
             near(prev_ref, part).start()
-    for index in indices:
+    for turn in range(2):
+        index = first if turn == 0 else 1 - first
+        slot = flip_low + index * (flip_high - flip_low)
         for part in parts:
-            far(own_ref, index, part).wait_recv()
-            onward(index, part).start()
+            arrived(index, slot, part).wait_recv()
+            onward(index, slot, part).start()
+            @pl.when(late == turn)
+            def _():
+                across(part).start()
+    for part in parts:
+        across(part).wait_recv()
+        onward(2, flip_both, part).start()
     for part in parts:
         near(own_ref, part).wait_recv()
-        for index in indices:
-            onward(index, part).wait_recv()
+        for index in range(3):
+            onward(index, r, part).wait_recv()
     coef_copy.wait()
     tail_copy.wait_send()
     for part in parts:
@@ -194,9 +226,11 @@
         def _():
             along(part).wait_send()
         near(own_ref, part).wait_send()
+        across(part).wait_send()
         for index in indices:
             far(own_ref, index, part).wait_send()
-            onward(index, part).wait_send()
+        for index in range(3):
+            onward(index, r, part).wait_send()
     own_copy.wait()
 
 
@@ -207,11 +241,9 @@
     rows = parent_keys.shape[0]
     codes = child_phase.shape[0]
     tiles = 2 * (-(-half_width // LANES))
-    wanted = (jnp.arange(codes, dtype=jnp.int32)[:, None] + codes * parent_keys[None, :]).reshape(-1, 1)
     slots = vlist_src.shape[1]
     fixed = slots // 2 // CHUNK * CHUNK
     padded = -(-slots // CHUNK) * CHUNK
-    others = group // 2 - 1
     dma = pltpu.SemaphoreType.DMA
     anywhere = pl.BlockSpec(memory_space=pl.ANY)
     vmem = pl.BlockSpec(memory_space=pltpu.VMEM)
@@ -231,7 +263,7 @@
         in_specs=[vmem] * 5 + [anywhere] * 3,
         out_specs=[vmem, anywhere, anywhere, anywhere, vmem, vmem, vmem],
         scratch_shapes=[
-            pltpu.VMEM(leaf_spectra.shape, leaf_spectra.dtype),
+            pltpu.VMEM(leaf_spectra.shape[::-1], leaf_spectra.dtype),
             pltpu.VMEM(coarsen.shape, coarsen.dtype),
             pltpu.VMEM(transfer.shape, transfer.dtype),
             pltpu.VMEM((2, tiles // 2 * LANES), jnp.float32),
@@ -241,9 +273,10 @@
             pltpu.VMEM((16, tiles, LANES), jnp.float32),
             pltpu.VMEM(coef, jnp.bfloat16),
             dma((PARTS,)), dma((PARTS,)),
-            dma((others, PARTS)), dma((others, PARTS)),
+            dma((2, PARTS)), dma((2, PARTS)),
             dma((PARTS,)), dma((PARTS,)),
-            dma((others, PARTS)), dma((others, PARTS)),
+            dma((3, PARTS)), dma((3, PARTS)),
+            dma((PARTS,)), dma((PARTS,)),
             dma, dma, dma, dma, dma, dma, dma,
         ],
         compiler_params=pltpu.CompilerParams(
@@ -251,26 +284,29 @@
         ),
         name="upward_and_window",
     )(
-        leaf_keys.reshape(1, -1), wanted, child_phase, vlist_src, vlist_type, leaf_spectra, coarsen, transfer
+        leaf_keys.reshape(1, -1), parent_keys.reshape(1, -1), child_phase, vlist_src, vlist_type, leaf_spectra.T, coarsen, transfer
     )
     return upward, window, coef, src, kind, more, fixed
 
 
-def interact_kernel(fixed, chunk, half_width, count_ref, src_ref, kind_ref, table, coef, out_ref, sums):
+def interact_kernel(fixed, chunk, half_width, count_ref, src_ref, kind_ref, table, coef, up_hbm, out_ref, up_out, sums, up_sem):
+    up_copy = pltpu.make_async_copy(up_hbm, up_out, up_sem)
+    up_copy.start()
     rows = table.shape[1]
     half = rows // 2
     most = (src_ref.shape[1] - fixed) // chunk
 
     def some_slots(target, count):
-        re = jnp.zeros((half, LANES), jnp.float32)
-        im = jnp.zeros((half, LANES), jnp.float32)
+        re = [jnp.zeros((half, LANES), jnp.float32)] * CHAINS
+        im = [jnp.zeros((half, LANES), jnp.float32)] * CHAINS
         for slot in range(count):
             source = table[src_ref[target, slot]].astype(jnp.float32)
             factor = coef[kind_ref[target, slot]].astype(jnp.float32)
-            re = re + (factor[:half] * source[:half] - factor[half:] * source[half:])
-            im = im + (factor[:half] * source[half:] + factor[half:] * source[:half])
-        sums[target, :half] = re
-        sums[target, half:] = im
+            i = slot % CHAINS
+            re[i] = re[i] + (factor[:half] * source[:half] - factor[half:] * source[half:])
+            im[i] = im[i] + (factor[:half] * source[half:] + factor[half:] * source[:half])
+        sums[target, :half] = sum(re[1:], re[0])
+        sums[target, half:] = sum(im[1:], im[0])
 
     def one_target(target, carry):
         def between(low, high):
@@ -289,34 +325,38 @@
         pieces = [sums[:, part * half + i, :] for i in range(half)]
         whole = jnp.concatenate(pieces, 1)[:, :half_width]
         out_ref[:, part * half_width : (part + 1) * half_width] = whole.astype(out_ref.dtype)
-
-
-def interact(window, coef, src, kind, more, fixed, half_width):
+    up_copy.wait()
+
+
+def interact(window, coef, src, kind, more, fixed, upward):
     targets = src.shape[0]
     smem = pl.BlockSpec(memory_space=pltpu.SMEM)
     vmem = pl.BlockSpec(memory_space=pltpu.VMEM)
+    anywhere = pl.BlockSpec(memory_space=pl.ANY)
     return pl.pallas_call(
-        functools.partial(interact_kernel, fixed, CHUNK, half_width),
-        out_shape=jax.ShapeDtypeStruct((targets, 2 * half_width), jnp.bfloat16),
-        in_specs=[smem, smem, smem, vmem, vmem],
-        out_specs=vmem,
-        scratch_shapes=[pltpu.VMEM((targets, window.shape[1], LANES), jnp.float32)],
+        functools.partial(interact_kernel, fixed, CHUNK, upward.shape[1] // 2),
+        out_shape=[jax.ShapeDtypeStruct(upward.shape, jnp.bfloat16)] * 2,
+        in_specs=[smem, smem, smem, vmem, vmem, anywhere],
+        out_specs=[vmem, anywhere],
+        scratch_shapes=[
+            pltpu.VMEM((targets, window.shape[1], LANES), jnp.float32),
+            pltpu.SemaphoreType.DMA,
+        ],
         compiler_params=pltpu.CompilerParams(vmem_limit_bytes=56 * 2**20),
         name="interact",
-    )(more, src, kind, window, coef)
+    )(more, src, kind, window, coef, upward)
 
 
 def shards(
     leaf_spectra, leaf_keys, parent_keys, child_phase, coarsen, transfer, vlist_src, vlist_type
 ):
-    half_width = child_phase.shape[1]
     group = 2**GBITS
     upward, window, coef, src, kind, more, fixed = upward_and_window(
         leaf_spectra, leaf_keys, parent_keys, child_phase, coarsen, transfer, vlist_src, vlist_type, "oct", group
     )
     rows = parent_keys.shape[0]
     window = window.reshape((group * rows,) + window.shape[2:])
-    local_field = interact(window, coef, src, kind, more, fixed, half_width)
+    local_field, upward = interact(window, coef, src, kind, more, fixed, upward)
     return (upward, local_field)
 
 

time: 63 us -> 65 us (1.032)
  Pallas kernels: 57.6 us -> 64 us
  local copies, waits for them, and re-layouts: 3.88 us -> 0 us
  other arithmetic: 0.67 us -> 0 us
    pallas_call x1, Pallas kernels: 27.8 us -> 36.7 us  [interact(): pl.pallas_call(functools.partial(interact_kernel, fixed, CHUNK, upward.sh...]
    unnamed x4 -> x0, local copies, waits for them, and re-layouts: 2.98 us -> none
    pallas_call x1, Pallas kernels: 29.9 us -> 27.3 us  [upward_and_window(): pl.pallas_call(functools.partial(upward_kernel, axis, lax.axis_size(axis)...]
    add x1 -> x0, local copies, waits for them, and re-layouts: 0.91 us -> none  [upward_and_window(): jnp.arange(codes, dtype=jnp.int32)[:, None] + codes * parent_keys[None, :]]
    mul x1 -> x0, other arithmetic: 0.66 us -> none  [upward_and_window(): codes * parent_keys[None, :]]
where the time goes in v5:
time: 65 us; the launch traced here: 64.6 us
  Pallas kernels  64 us (98%)
    pallas_call x1, Pallas kernels, interact(): pl.pallas_call(functools.partial(interact_kernel, fixed, CHUNK, upward.sh...  36.7 us
    pallas_call x1, Pallas kernels, upward_and_window(): pl.pallas_call(functools.partial(upward_kernel, axis, lax.axis_size(axis)...  27.3 us

profile of v5, /device:TPU:1, one launch (start us, length us, event | category | flops | bytes accessed | tf_op | source)
XLA Modules:
  0.0 64.6 jit_solution(15503703480100472938)
XLA Ops:
  0.6 27.3 %upward_and_window.1 = (bf16[64,2016]{1,0:T(8,128)(2,1)}, bf16[8,64,16,128]{3,2,1,0:T(8,128)(2,1)}, bf16[64,16,128]{2,1,0:T(8,128)(2,1)}, bf16[317,16,128]{2,1,0...) custom-call(s32[1,256]{1,0:T(1,128)} %bitcast.6, s32[1,64]{1,0:T(1,128)} %bitcast.7, ...), custom_call_target="tpu_custom_call" | custom-call | tf_op jit(solution)/shard_map/upward_and_window/pallas_call | solution.py:252
  27.9 36.7 %interact.1 = (bf16[64,2016]{1,0:T(8,128)(2,1)}, bf16[64,2016]{1,0:T(8,128)(2,1)}) custom-call(s32[64,1]{1,0:T(8,128)} %get-tuple-element.10.count_ref, s32[64,192]{1,0:T(8,128)} %get-tuple-element.11.src_ref, s32[64,192]{1,0:T(8,128)} %get-tuple-element.12.kind_ref, bf16[512,16,128]{2,1,0:T(8,128)(2,1)} %bitcast.4, ...), custom_call_target="tpu_custom_call" | custom-call | tf_op jit(solution)/shard_map/interact/pallas_call | solution.py:336

commit v6 on v5

--- a/solution.py
+++ b/solution.py
@@ -10,7 +10,6 @@
 LANES = 128
 CHUNK = 16
 PARTS = 4
-CHAINS = 4
 
 
 def upward_kernel(
@@ -289,24 +288,22 @@
     return upward, window, coef, src, kind, more, fixed
 
 
-def interact_kernel(fixed, chunk, half_width, count_ref, src_ref, kind_ref, table, coef, up_hbm, out_ref, up_out, sums, up_sem):
-    up_copy = pltpu.make_async_copy(up_hbm, up_out, up_sem)
-    up_copy.start()
+def interact_kernel(fixed, chunk, half_width, count_ref, src_ref, kind_ref, table, coef, up_ref, out_ref, up_out, sums):
+    up_out[...] = up_ref[...]
     rows = table.shape[1]
     half = rows // 2
     most = (src_ref.shape[1] - fixed) // chunk
 
     def some_slots(target, count):
-        re = [jnp.zeros((half, LANES), jnp.float32)] * CHAINS
-        im = [jnp.zeros((half, LANES), jnp.float32)] * CHAINS
+        re = jnp.zeros((half, LANES), jnp.float32)
+        im = jnp.zeros((half, LANES), jnp.float32)
         for slot in range(count):
             source = table[src_ref[target, slot]].astype(jnp.float32)
             factor = coef[kind_ref[target, slot]].astype(jnp.float32)
-            i = slot % CHAINS
-            re[i] = re[i] + (factor[:half] * source[:half] - factor[half:] * source[half:])
-            im[i] = im[i] + (factor[:half] * source[half:] + factor[half:] * source[:half])
-        sums[target, :half] = sum(re[1:], re[0])
-        sums[target, half:] = sum(im[1:], im[0])
+            re = re + (factor[:half] * source[:half] - factor[half:] * source[half:])
+            im = im + (factor[:half] * source[half:] + factor[half:] * source[:half])
+        sums[target, :half] = re
+        sums[target, half:] = im
 
     def one_target(target, carry):
         def between(low, high):
@@ -325,23 +322,18 @@
         pieces = [sums[:, part * half + i, :] for i in range(half)]
         whole = jnp.concatenate(pieces, 1)[:, :half_width]
         out_ref[:, part * half_width : (part + 1) * half_width] = whole.astype(out_ref.dtype)
-    up_copy.wait()
 
 
 def interact(window, coef, src, kind, more, fixed, upward):
     targets = src.shape[0]
     smem = pl.BlockSpec(memory_space=pltpu.SMEM)
     vmem = pl.BlockSpec(memory_space=pltpu.VMEM)
-    anywhere = pl.BlockSpec(memory_space=pl.ANY)
     return pl.pallas_call(
         functools.partial(interact_kernel, fixed, CHUNK, upward.shape[1] // 2),
         out_shape=[jax.ShapeDtypeStruct(upward.shape, jnp.bfloat16)] * 2,
-        in_specs=[smem, smem, smem, vmem, vmem, anywhere],
-        out_specs=[vmem, anywhere],
-        scratch_shapes=[
-            pltpu.VMEM((targets, window.shape[1], LANES), jnp.float32),
-            pltpu.SemaphoreType.DMA,
-        ],
+        in_specs=[smem, smem, smem, vmem, vmem, vmem],
+        out_specs=[vmem, vmem],
+        scratch_shapes=[pltpu.VMEM((targets, window.shape[1], LANES), jnp.float32)],
         compiler_params=pltpu.CompilerParams(vmem_limit_bytes=56 * 2**20),
         name="interact",
     )(more, src, kind, window, coef, upward)

time: 65 us -> 56.4 us (0.87)
  the two profiles are of different devices: /device:TPU:1 before, /device:TPU:5 now
where the time goes in v6:
time: 56.4 us; the launch traced here: 56.1 us
  Pallas kernels  55.4 us (98%)
  between operations  0.64 us (1%)
    pallas_call x1, Pallas kernels, upward_and_window(): pl.pallas_call(functools.partial(upward_kernel, axis, lax.axis_size(axis)...  28 us
    pallas_call x1, Pallas kernels, interact(): pl.pallas_call(functools.partial(interact_kernel, fixed, CHUNK, upward.sh...  27.4 us

profile of v6, /device:TPU:5, one launch (start us, length us, event | category | flops | bytes accessed | tf_op | source)
XLA Modules:
  0.0 56.1 jit_solution(8823525948272046966)
XLA Ops:
  0.6 28.0 %upward_and_window.1 = (bf16[64,2016]{1,0:T(8,128)(2,1)}, bf16[8,64,16,128]{3,2,1,0:T(8,128)(2,1)}, bf16[64,16,128]{2,1,0:T(8,128)(2,1)}, bf16[317,16,128]{2,1,0...) custom-call(s32[1,256]{1,0:T(1,128)} %bitcast.6, s32[1,64]{1,0:T(1,128)} %bitcast.7, ...), custom_call_target="tpu_custom_call" | custom-call | tf_op jit(solution)/shard_map/upward_and_window/pallas_call | solution.py:251
  28.6 27.4 %interact.1 = (bf16[64,2016]{1,0:T(8,128)(2,1)}, bf16[64,2016]{1,0:T(8,128)(2,1)}) custom-call(s32[64,1]{1,0:T(8,128)} %get-tuple-element.10.count_ref, s32[64,192]{1,0:T(8,128)} %get-tuple-element.11.src_ref, s32[64,192]{1,0:T(8,128)} %get-tuple-element.12.kind_ref, bf16[512,16,128]{2,1,0:T(8,128)(2,1)} %bitcast.4, ...), custom_call_target="tpu_custom_call" | custom-call | tf_op jit(solution)/shard_map/interact/pallas_call | solution.py:331
